TPU v7x, 32 devices: a whole 2x2x4 slice. The times are simulated.
32 devices in a mesh: grp: 4 (over y, x), mem: 8 (over z, core).
Axes of the slice: x: 2, y: 2, z: 4, core: 2. Of those that a mesh axis runs over, the one named last changes fastest.
Arguments:
- t_amps: bfloat16 [320, 32, 600], P(('grp', 'mem')), may hold values from -6 to 6
- vvvv: bfloat16 [19200, 9600], P('mem', 'grp'), may hold values from -0.125 to 0.125
- irreps: int32 [600], replicated, may hold values from 0 to 7
Outputs:
- ladder: float32 [320, 9600], P('mem', 'grp')
All inputs are finite; a program needn't handle non-finite values.
Results may differ from a plain program's by a relative error of at most 0.0003.
Values may be sent and summed in bfloat16 or wider, within the bound.
No kernel may reach another device: no remote copies, remote signals or barrier semaphores. Data moves between devices by JAX's collectives and lax.ppermute only.
A program may use at most 128 MiB of HBM per device.

v0:
```python
import jax
import jax.numpy as jnp
from jax import lax
from jax.sharding import PartitionSpec as P

NV = 600


def shards(t_amps, vvvv, irreps):
    mem_count = lax.axis_size("mem")
    grp_count = lax.axis_size("grp")
    per_device = t_amps.shape[0]
    c_local = vvvv.shape[0] // NV
    a_local = vvvv.shape[1] // NV
    spread = lax.all_to_all(t_amps, "mem", split_axis=1, concat_axis=0, tiled=True)
    gathered = lax.all_gather(spread, "grp", axis=0, tiled=True)
    total_pairs = per_device * mem_count * grp_count
    amps = gathered.reshape(total_pairs, c_local * NV)
    mem_index = lax.axis_index("mem")
    grp_index = lax.axis_index("grp")
    c_labels = lax.dynamic_slice_in_dim(irreps, mem_index * c_local, c_local, 0)
    a_labels = lax.dynamic_slice_in_dim(irreps, grp_index * a_local, a_local, 0)
    pair_c = jnp.bitwise_xor(c_labels[:, None], irreps[None, :]).reshape(-1)
    pair_a = jnp.bitwise_xor(a_labels[:, None], irreps[None, :]).reshape(-1)
    masked = jnp.where(pair_c[:, None] == pair_a[None, :], vvvv, jnp.zeros((), vvvv.dtype))
    partial_sum = jnp.dot(amps, masked, preferred_element_type=jnp.float32)
    return lax.psum_scatter(partial_sum, "mem", scatter_dimension=0, tiled=True)


def solution(mesh):
    in_specs = (P(("grp", "mem"), None, None), P("mem", "grp"), P())
    out_specs = P("mem", "grp")
    return jax.shard_map(shards, mesh=mesh, in_specs=in_specs, out_specs=out_specs, check_vma=False)
```

profile of v0, /device:TPU:0, one launch (start us, length us, event | category | flops | bytes accessed | tf_op | source)
XLA Modules:
  0.0 124.7 jit_solution(12036630121183605407)
XLA Ops:
  6.5 0.0 all-gather.2.cloned.1.call-start
  6.5 1.1 copy.5
  7.7 24.3 %all_to_all.18 = bf16[10,32,600]{2,0,1:T(8,128)(2,1)S(1)} all-to-all(bf16[10,32,600]{2,0,1:T(8,128)(2,1)S(1)} %copy.5), channel_id=1, replica_groups=mesh['grp'=4,'mem'=8] {'mem'}, dimensions={1} | all-to-all | bytes 768000 | tf_op jit(solution)/shard_map/all_to_all | solution.py:15
  32.0 0.9 copy.6
  32.9 0.0 all-gather.2.cloned.1.call-update
  32.9 0.0 reduce-scatter.4.cloned.1.call-start
  33.0 0.8 fusion.6
  33.8 0.8 broadcast_xor_fusion.1
  34.6 0.1 xor.41
  34.6 0.1 xor.44
  34.7 28.8 %all-gather.2.cloned.1.call-done = bf16[320,4,600]{2,1,0:T(4,128)(2,1)} async-done(((bf16[80,4,600]{2,1,0:T(4,128)(2,1)}), bf16[320,4,600]{2,1,0:T(4,128)(2,1)}) %all-gather.2.cloned.1.call-update) | async-done | bytes 1536016 | tf_op jit(solution)/shard_map/all_gather | solution.py:16
  63.5 3.0 %reshape.34 = bf16[320,2400]{1,0:T(8,128)(2,1)S(1)} reshape(bf16[320,4,600]{2,1,0:T(4,128)(2,1)} %all-gather.2.cloned.1.call-done) | data formatting | bytes 3072000 | tf_op jit(solution)/shard_map/reshape | solution.py:18
  66.5 10.9 %fusion.4 = f32[320,2400]{1,0:T(8,128)} fusion(bf16[320,2400]{1,0:T(8,128)(2,1)S(1)} %reshape.34, bf16[2400,2400]{1,0:T(8,128)(2,1)} %param.4, s32[2400]{0:T(1024)S(1)} %xor.44, s32[2400]{0:T(1024)S(1)} %xor.41), kind=kOutput, calls=%fused_computation.5 | convolution fusion | flops 3697920000 | bytes 16147200 | tf_op jit(solution)/shard_map/dot_general | solution.py:26
  77.4 0.0 reduce-scatter.4.cloned.1.call-update
  77.4 40.4 %reduce-scatter.4.cloned.1.call-done = f32[40,2400]{1,0:T(8,128)} async-done(((f32[320,2400]{1,0:T(8,128)}), f32[40,2400]{1,0:T(8,128)}) %reduce-scatter.4.cloned.1.call-update) | async-done | bytes 384016
Async XLA Ops:
  6.5 57.0 %all-gather.2.cloned.1.call-start = ((), (), s32[]{:S(2)}) async-start(), calls=%async_computation.2 | async-start | bytes 2048000 | tf_op jit(solution)/shard_map/all_gather | solution.py:16
  32.9 85.0 %reduce-scatter.4.cloned.1.call-start = ((), (), s32[]{:S(2)}) async-start(), calls=%async_computation.3 | async-start | bytes 3502080
Sparse Core Ops, SparseCore 0:
  33.0 30.4 all-gather.1
  77.5 40.2 reduce-scatter.3
where the time goes:
time: 125 us
  waiting for transfers between devices  69.2 us (55%)
  blocking collectives  24.3 us (19%)
  between operations  13.4 us (11%)
  matrix products  10.9 us (9%)
  local copies, waits for them, and re-layouts  6.05 us (5%)
    unnamed x3, waiting for transfers between devices  40.5 us
    all_gather x1, waiting for transfers between devices, shards(): gathered = lax.all_gather(spread, 'grp', axis=0, tiled=True)  28.8 us
    all_to_all x1, blocking collectives, shards(): lax.all_to_all(t_amps, 'mem', split_axis=1, concat_axis=0, tiled=True)  24.3 us
    dot_general x1, matrix products, shards(): partial_sum = jnp.dot(amps, masked, preferred_element_type=jnp.float32)  10.9 us
    reshape x1, local copies, waits for them, and re-layouts, shards(): amps = gathered.reshape(total_pairs, c_local * NV)  3.01 us
  transfers between devices with their start and end apart: 2, of which 2 were waited for; matrix products, arithmetic and copies ran while one was open for 1% of the time, Pallas kernels for 0%

commit v1 on v0

v1 whole, which is shorter than its diff:
```python
import jax
import jax.numpy as jnp
from jax import lax
from jax.experimental import pallas as pl
from jax.experimental.pallas import tpu as pltpu
from jax.sharding import PartitionSpec as P

LANES = 128
TILE_N = 512
QMAX = 32000.0
STEPS = 8.0


def round_up(value, unit):
    return -(-value // unit) * unit


def partial_kernel(shape, where_ref, *refs):
    grp_count, chips, cc, nv, width = shape
    lhs_refs = refs[:grp_count]
    v_ref, w_ref, row_ref, col_ref, code_ref, own_ref, wide, lhs, masked, scales = refs[grp_count:]
    step = pl.program_id(0)
    group, chip, core = where_ref[0], where_ref[1], where_ref[2]
    rows_each = lhs_refs[0].shape[0]
    half = cc // 2
    depth = masked.shape[1]
    block = code_ref.shape[1]

    @pl.when(step == 0)
    def _():
        for j in range(grp_count):
            wide[j * rows_each:(j + 1) * rows_each, :] = lhs_refs[j][...].astype(jnp.float32)
        lhs[...] = wide[...].astype(jnp.bfloat16)
        masked[...] = jnp.zeros_like(masked)
        scales[...] = jnp.zeros_like(scales)

    for side, source in ((core, v_ref), (1 - core, w_ref)):
        for c in range(half):
            at = side * half + c
            labels = row_ref[at]
            for n in range(0, TILE_N, LANES):
                keep = labels == col_ref[0:1, n:n + LANES]
                masked[at, 0:nv, n:n + LANES] = jnp.where(keep, source[c, :, n:n + LANES], jnp.zeros((), jnp.bfloat16))
    total = jnp.dot(lhs[...], masked[...].reshape(cc * depth, TILE_N), preferred_element_type=jnp.float32)

    lane = lax.broadcasted_iota(jnp.int32, (total.shape[0], LANES), 1)
    exponents = scales[...]
    first = step * (TILE_N // LANES)
    coded = []
    for n in range(0, TILE_N, LANES):
        part = total[:, n:n + LANES]
        top = jnp.maximum(jnp.max(jnp.abs(part), axis=1, keepdims=True), 1e-30)
        level = jnp.ceil(jnp.log2(top) * STEPS + 0.05)
        code = jnp.round(part * (jnp.exp2(level * (-1.0 / STEPS)) * QMAX))
        at = first + n // LANES
        exponents = jnp.where(lane == width % LANES + at, level, exponents)
        is_last = at == width // LANES
        code = jnp.where(jnp.logical_and(is_last, lane >= width % LANES), exponents, code)
        coded.append(code)
    scales[...] = exponents
    per_group = rows_each // block
    for j in range(grp_count):
        for q in range(per_group):
            low = j * rows_each + q * block
            target = jnp.bitwise_xor(jnp.bitwise_xor(group, j) * per_group + q, chip)
            for i, n in enumerate(range(0, TILE_N, LANES)):
                code_ref[target, :, n:n + LANES] = coded[i][low:low + block].astype(jnp.int16)

            @pl.when(target == 0)
            def _():
                own_ref[...] = total[low:low + block]


def combine_kernel(width, own_ref, *refs):
    code_refs, out_ref = refs[:-1], refs[-1]
    base = width // LANES * LANES
    exponents = [jnp.exp2(ref[:, base:base + LANES].astype(jnp.float32) * (1.0 / STEPS)) * (1.0 / QMAX) for ref in code_refs]
    for low in range(0, width, LANES):
        high = min(low + LANES, width)
        at = width % LANES + low // LANES
        value = own_ref[:, low:high]
        for scale, ref in zip(exponents, code_refs):
            value = value + ref[:, low:high].astype(jnp.float32) * scale[:, at:at + 1]
        out_ref[:, low:high] = value


def shards(t_amps, vvvv, irreps):
    mem_count = lax.axis_size("mem")
    grp_count = lax.axis_size("grp")
    per_device, cw, nv = t_amps.shape
    chips = mem_count // 2
    cc = cw // chips
    half = cc // 2
    width = vvvv.shape[1]
    a_local = width // nv
    mem = lax.axis_index("mem")
    group = lax.axis_index("grp")
    chip, core = mem // 2, mem % 2

    def swap(x, axis, k, count):
        return lax.ppermute(x, axis, [(i, i ^ k) for i in range(count)])

    other = swap(vvvv, "mem", 1, mem_count)

    depth = round_up(nv, LANES)
    padded = jnp.pad(t_amps, ((0, 0), (0, 0), (0, depth - nv))).reshape(per_device, chips, cc, depth)

    def slot(m):
        return m // (2 * grp_count) * grp_count + m % grp_count

    pieces = []
    for r in range(chips):
        send = lax.dynamic_index_in_dim(padded, jnp.bitwise_xor(slot(mem), r), 1, keepdims=False)
        perm = [(m, (slot(m) ^ r) * 2 + m // grp_count % 2) for m in range(mem_count)]
        pieces.append(lax.ppermute(send, "mem", perm))
    bit = 1
    while bit < chips:
        flip = jnp.bitwise_and(chip, bit) != 0
        pieces = [jnp.where(flip, pieces[j ^ bit], pieces[j]) for j in range(chips)]
        bit *= 2
    mine = jnp.concatenate(pieces).reshape(chips * per_device, cc * depth)

    near = swap(mine, "grp", 1, grp_count)
    far = swap(mine, "grp", 2, grp_count)
    cut = cc * depth // 2
    corner = jnp.concatenate([swap(near[:, :cut], "grp", 2, grp_count), swap(far[:, cut:], "grp", 1, grp_count)], axis=1)
    lhs = [mine, near, far, corner]

    c_labels = lax.dynamic_slice_in_dim(irreps, chip * cc, cc, 0)
    a_labels = lax.dynamic_slice_in_dim(irreps, group * a_local, a_local, 0)
    pair_c = jnp.bitwise_xor(c_labels[:, None], irreps[None, :]).astype(jnp.bfloat16)
    pair_a = jnp.bitwise_xor(a_labels[:, None], irreps[None, :]).reshape(-1).astype(jnp.bfloat16)
    row_labels = jnp.broadcast_to(pair_c[:, :, None], (cc, nv, LANES))
    steps = -(-width // TILE_N)
    col_labels = jnp.full((1, steps * TILE_N), -1, jnp.bfloat16).at[0, :width].set(pair_a)
    col_labels = jnp.broadcast_to(col_labels, (16, steps * TILE_N))

    rows = grp_count * chips * per_device
    block = grp_count * per_device
    coded_width = round_up(width, LANES)
    where = jnp.stack([group, chip, core]).astype(jnp.int32)
    whole = lambda shape: pl.BlockSpec(shape, lambda i: (0,) * len(shape))
    codes, own = pl.pallas_call(
        lambda *refs: partial_kernel((grp_count, chips, cc, nv, width), *refs),
        grid=(steps,),
        in_specs=[pl.BlockSpec(memory_space=pltpu.SMEM)]
        + [whole((chips * per_device, cc * depth))] * grp_count
        + [pl.BlockSpec((half, nv, TILE_N), lambda i: (0, 0, i))] * 2
        + [whole((cc, nv, LANES)), pl.BlockSpec((16, TILE_N), lambda i: (0, i))],
        out_specs=[
            pl.BlockSpec((chips, block, TILE_N), lambda i: (0, 0, i)),
            pl.BlockSpec((block, TILE_N), lambda i: (0, i)),
        ],
        out_shape=[
            jax.ShapeDtypeStruct((chips, block, coded_width), jnp.int16),
            jax.ShapeDtypeStruct((block, width), jnp.float32),
        ],
        scratch_shapes=[
            pltpu.VMEM((rows, cc * depth), jnp.float32),
            pltpu.VMEM((rows, cc * depth), jnp.bfloat16),
            pltpu.VMEM((cc, depth, TILE_N), jnp.bfloat16),
            pltpu.VMEM((rows, LANES), jnp.float32),
        ],
        compiler_params=pltpu.CompilerParams(vmem_limit_bytes=60 * 2**20),
    )(where, *lhs, vvvv.reshape(half, nv, width), other.reshape(half, nv, width), row_labels, col_labels)

    arrived = [swap(codes[r], "mem", 2 * r, mem_count) for r in range(1, chips)]
    return pl.pallas_call(
        lambda *refs: combine_kernel(width, *refs),
        out_shape=jax.ShapeDtypeStruct((block, width), jnp.float32),
        compiler_params=pltpu.CompilerParams(vmem_limit_bytes=32 * 2**20),
    )(own, *arrived)


def solution(mesh):
    in_specs = (P(("grp", "mem"), None, None), P("mem", "grp"), P())
    out_specs = P("mem", "grp")
    return jax.shard_map(shards, mesh=mesh, in_specs=in_specs, out_specs=out_specs, check_vma=False)
```

time: 125 us -> 83.1 us (0.66)
  waiting for transfers between devices: 69.2 us -> 26.9 us
  blocking collectives: 24.3 us -> 0 us
  starting transfers between devices: 0.04 us -> 24.2 us
  Pallas kernels: 0 us -> 19.9 us
  between operations: 13.4 us -> 0.11 us
  matrix products: 10.9 us -> 0 us
  other arithmetic: 0.76 us -> 4.34 us
    unnamed x3 -> x0, waiting for transfers between devices: 40.5 us -> none
    all_gather x1 -> x0, waiting for transfers between devices: 28.8 us -> none  [shards(): gathered = lax.all_gather(spread, 'grp', axis=0, tiled=True)]
    ppermute x0 -> x12, waiting for transfers between devices: none -> 26.9 us  [the longest x8 23.5 us: swap(): return lax.ppermute(x, axis, [(i, i ^ k) for i in range(count)])]
    all_to_all x1 -> x0, blocking collectives: 24.3 us -> none  [shards(): lax.all_to_all(t_amps, 'mem', split_axis=1, concat_axis=0, tiled=True)]
    ppermute x0 -> x12, starting transfers between devices: none -> 24.2 us  [the longest x4 12.6 us: shards(): pieces.append(lax.ppermute(send, 'mem', perm))]
    pallas_call x0 -> x2, Pallas kernels: none -> 19.9 us  [the longest x1 18.8 us: shards(): pl.pallas_call(lambda *refs: partial_kernel((grp_count, chips, cc, nv, wi...]
    dot_general x1 -> x0, matrix products: 10.9 us -> none  [shards(): partial_sum = jnp.dot(amps, masked, preferred_element_type=jnp.float32)]
    broadcast_in_dim x0 -> x3, local copies, waits for them, and re-layouts: none -> 2.37 us  [the longest x1 1.64 us: shards(): row_labels = jnp.broadcast_to(pair_c[:, :, None], (cc, nv, LANES))]
  transfers between devices with their start and end apart: 2 -> 12, of which waited for: 2 -> 6; matrix products, arithmetic and copies ran while one was open for 1% -> 9% of each run, Pallas kernels for 0% -> 0%
where the time goes in v1:
time: 83.1 us; the launch traced here: 82.7 us
  waiting for transfers between devices  26.9 us (32%)
  starting transfers between devices  24.2 us (29%)
  Pallas kernels  19.9 us (24%)
  local copies, waits for them, and re-layouts  7.23 us (9%)
  other arithmetic  4.34 us (5%)
    ppermute x8, waiting for transfers between devices, swap(): return lax.ppermute(x, axis, [(i, i ^ k) for i in range(count)])  23.5 us
    pallas_call x1, Pallas kernels, shards(): pl.pallas_call(lambda *refs: partial_kernel((grp_count, chips, cc, nv, wi...  18.8 us
    ppermute x4, starting transfers between devices, shards(): pieces.append(lax.ppermute(send, 'mem', perm))  12.6 us
    ppermute x8, starting transfers between devices, swap(): return lax.ppermute(x, axis, [(i, i ^ k) for i in range(count)])  11.6 us
    ppermute x4, waiting for transfers between devices, shards(): pieces.append(lax.ppermute(send, 'mem', perm))  3.38 us
  transfers between devices with their start and end apart: 12, of which 6 were waited for; matrix products, arithmetic and copies ran while one was open for 9% of the time, Pallas kernels for 0%

profile of v1, /device:TPU:0, one launch (start us, length us, event | category | flops | bytes accessed | tf_op | source)
XLA Modules:
  0.0 82.7 jit_solution(15704613231136704799)
XLA Ops:
  0.5 1.0 %pad_bitcast_fusion = bf16[10,4,8,640]{3,2,1,0:T(8,128)(2,1)S(1)} fusion(bf16[10,32,600]{2,1,0:T(8,128)(2,1)} %param.5), kind=kLoop, calls=%fused_computation.2 | loop fusion | bytes 793600 | tf_op jit(solution)/shard_map/reshape | solution.py:106
  1.6 2.6 %collective-permute-start.2 = (bf16[10,8,640]{2,1,0:T(8,128)(2,1)S(1)}, bf16[10,8,640]{2,1,0:T(8,128)(2,1)S(1)}, u32[]{:S(2)}, u32[]{:S(2)}) collective-permute-start(bf16[10,8,640]{2,1,0:T(8,128)(2,1)S(1)} %get-tuple-element.28), channel_id=1, source_target_pairs={{0,2},{1,0},{2,6},{3,4},{4,3},{5,1},{6,7},{7,5},{8,10},{9,8},{10,1... | collective-permute-start | bytes 307208 | tf_op jit(solution)/shard_map/ppermute | solution.py:115
  4.2 0.7 collective-permute-start.3
  4.9 2.9 %collective-permute-start.1 = (bf16[10,8,640]{2,1,0:T(8,128)(2,1)S(1)}, bf16[10,8,640]{2,1,0:T(8,128)(2,1)S(1)}, u32[]{:S(2)}, u32[]{:S(2)}) collective-permute-start(bf16[10,8,640]{2,1,0:T(8,128)(2,1)S(1)} %get-tuple-element.30), channel_id=1, source_target_pairs={{0,4},{1,6},{2,0},{3,2},{4,5},{5,7},{6,1},{7,3},{8,12},{9,14},{10,... | collective-permute-start | bytes 307208 | tf_op jit(solution)/shard_map/ppermute | solution.py:115
  7.7 6.4 %collective-permute-start = (bf16[10,8,640]{2,1,0:T(8,128)(2,1)S(1)}, bf16[10,8,640]{2,1,0:T(8,128)(2,1)S(1)}, u32[]{:S(2)}, u32[]{:S(2)}) collective-permute-start(bf16[10,8,640]{2,1,0:T(8,128)(2,1)S(1)} %get-tuple-element.31), channel_id=1, source_target_pairs={{0,6},{1,4},{2,2},{3,0},{4,7},{5,5},{6,3},{7,1},{8,14},{9,12},{10,... | collective-permute-start | bytes 307208 | tf_op jit(solution)/shard_map/ppermute | solution.py:115
  14.2 3.4 %collective-permute-done.2 = bf16[10,8,640]{2,1,0:T(8,128)(2,1)S(1)} collective-permute-done((bf16[10,8,640]{2,1,0:T(8,128)(2,1)S(1)}, bf16[10,8,640]{2,1,0:T(8,128)(2,1)S(1)}, u32[]{:S(2)}, u32[]{:S(2)}) %collective-permute-start.2) | collective-permute-done | bytes 102432 | tf_op jit(solution)/shard_map/ppermute | solution.py:115
  18.2 1.5 %collective-permute-start.4 = (bf16[40,5120]{1,0:T(8,128)(2,1)S(1)}, bf16[40,5120]{1,0:T(8,128)(2,1)S(1)}, u32[]{:S(2)}, u32[]{:S(2)}) collective-permute-start(bf16[40,5120]{1,0:T(8,128)(2,1)S(1)} %bitcast.25), channel_id=1, source_target_pairs={{0,8},{8,0},{16,24},{24,16},{1,9},{9,1},{17,25},{25,17},{2,10},{10... | collective-permute-start | bytes 1228808 | tf_op jit(solution)/shard_map/ppermute | solution.py:101
  19.7 0.8 dynamic_slice.23
  20.5 0.8 dynamic_slice.24
  21.9 1.4 %fusion = bf16[4,600]{1,0:T(4,128)(2,1)S(1)} fusion(s32[600]{0:T(1024)} %param.7, s32[4]{0:T(128)S(1)} %dynamic_slice.24, pred[]{:T(512)} %compare_reduce_fusion), kind=kLoop, calls=%fused_computation.20 | loop fusion | flops 7200 | bytes 7217 | tf_op jit(solution)/shard_map/broadcast_in_dim | solution.py:136
  24.0 5.4 %collective-permute-done.5.refs_3_ = bf16[40,5120]{1,0:T(8,128)(2,1)S(1)} collective-permute-done((bf16[40,5120]{1,0:T(8,128)(2,1)S(1)}, bf16[40,5120]{1,0:T(8,128)(2,1)S(1)}, u32[]{:S(2)}, u32[]{:S(2)}) %collective-permute-start.5) | collective-permute-done | bytes 409632 | tf_op jit(solution)/shard_map/ppermute | solution.py:101
  30.0 1.6 %collective-permute-start.6 = (bf16[40,2560]{1,0:T(8,128)(2,1)S(1)}, bf16[40,2560]{1,0:T(8,128)(2,1)S(1)}, u32[]{:S(2)}, u32[]{:S(2)}) collective-permute-start(bf16[40,2560]{1,0:T(8,128)(2,1)S(1)} %slice.36), channel_id=1, source_target_pairs={{0,16},{8,24},{16,0},{24,8},{1,17},{9,25},{17,1},{25,9},{2,18},{10... | collective-permute-start | bytes 614408 | tf_op jit(solution)/shard_map/ppermute | solution.py:101
  31.5 0.8 xor_convert_fusion
  32.3 3.4 %collective-permute-done.7 = bf16[40,2560]{1,0:T(8,128)(2,1)S(1)} collective-permute-done((bf16[40,2560]{1,0:T(8,128)(2,1)S(1)}, bf16[40,2560]{1,0:T(8,128)(2,1)S(1)}, u32[]{:S(2)}, u32[]{:S(2)}) %collective-permute-start.7) | collective-permute-done | bytes 204832 | tf_op jit(solution)/shard_map/ppermute | solution.py:101
  36.2 0.8 pad_maximum_fusion.1.refs_4_
  37.0 0.6 broadcast_in_dim.11.refs_8_
  37.7 1.6 %broadcast_in_dim.8.refs_7_ = bf16[8,600,128]{2,1,0:T(8,128)(2,1)} broadcast(bf16[8,600]{1,0:T(8,128)(2,1)S(1)} %xor_convert_fusion), dimensions={0,1} | broadcast | bytes 1238400 | tf_op jit(solution)/shard_map/broadcast_in_dim | solution.py:133
  39.3 18.8 %shard_map.37 = (s16[4,40,2432]{2,1,0:T(8,128)(2,1)}, f32[40,2400]{1,0:T(8,128)}) custom-call(s32[3]{0:T(128)} %pad_add_fusion.refs_0_, bf16[40,5120]{1,0:T(8,128)(2,1)} %bitcast.26, bf16[40,5120]{1,0:T(8,128)(2,1)} %copy-done.3, bf16[40,5120]{1,0:T(8,128)(2,1)} %copy-done.2, bf16[40,5120]{1,0:T(8,128)(2,1)} %pad_maximum_fusion.1.refs_4_, ...), custom_call_target="tpu_custom_call" | custom-call | tf_op jit(solution)/shard_map/pallas_call | solution.py:143
  58.1 1.2 %slice_bitcast_fusion = (s16[40,2432]{1,0:T(8,128)(2,1)S(1)}, s16[40,2432]{1,0:T(8,128)(2,1)S(1)}, s16[40,2432]{1,0:T(8,128)(2,1)S(1)}) fusion(s16[4,40,2432]{2,1,0:T(8,128)(2,1)} %get-tuple-element.20), kind=kLoop, calls=%fused_computation.3 | loop fusion | bytes 1167360 | tf_op jit(solution)/shard_map/squeeze | solution.py:167
  59.2 6.5 %collective-permute-start.11 = (s16[40,2432]{1,0:T(8,128)(2,1)S(1)}, s16[40,2432]{1,0:T(8,128)(2,1)S(1)}, u32[]{:S(2)}, u32[]{:S(2)}) collective-permute-start(s16[40,2432]{1,0:T(8,128)(2,1)S(1)} %get-tuple-element.21), channel_id=1, source_target_pairs={{0,6},{1,7},{2,4},{3,5},{4,2},{5,3},{6,0},{7,1},{8,14},{9,15},{10,... | collective-permute-start | bytes 583688 | tf_op jit(solution)/shard_map/ppermute | solution.py:101
  66.4 5.1 %collective-permute-done.11.refs_3_ = s16[40,2432]{1,0:T(8,128)(2,1)S(1)} collective-permute-done((s16[40,2432]{1,0:T(8,128)(2,1)S(1)}, s16[40,2432]{1,0:T(8,128)(2,1)S(1)}, u32[]{:S(2)}, u32[]{:S(2)}) %collective-permute-start.11) | collective-permute-done | bytes 194592 | tf_op jit(solution)/shard_map/ppermute | solution.py:101
  71.5 9.1 %collective-permute-done.10.refs_2_ = s16[40,2432]{1,0:T(8,128)(2,1)S(1)} collective-permute-done((s16[40,2432]{1,0:T(8,128)(2,1)S(1)}, s16[40,2432]{1,0:T(8,128)(2,1)S(1)}, u32[]{:S(2)}, u32[]{:S(2)}) %collective-permute-start.10) | collective-permute-done | bytes 194592 | tf_op jit(solution)/shard_map/ppermute | solution.py:101
  80.6 1.0 %copy-done = f32[40,2400]{1,0:T(8,128)S(1)} copy-done((f32[40,2400]{1,0:T(8,128)S(1)}, f32[40,2400]{1,0:T(8,128)}, u32[]{:S(2)}) %copy-start) | copy-done | bytes 384024
  81.6 1.2 %shard_map.38 = f32[40,2400]{1,0:T(8,128)} custom-call(f32[40,2400]{1,0:T(8,128)S(1)} %copy-done, s16[40,2432]{1,0:T(8,128)(2,1)S(1)} %collective-permute-done.9.refs_1_, s16[40,2432]{1,0:T(8,128)(2,1)S(1)} %collective-permute-done.10.refs_2_, s16[40,2432]{1,0:T(8,128)(2,1)S(1)} %collective-permute-done.11.refs_3_), custom_call_target="tpu_custom_call" | custom-call | tf_op jit(solution)/shard_map/pallas_call | solution.py:168
  (29 shorter events, 4.2 us)
Async XLA Ops:
  0.0 37.0 %collective-permute-start.8 = (bf16[2400,2400]{1,0:T(8,128)(2,1)}, bf16[2400,2400]{1,0:T(8,128)(2,1)}, u32[]{:S(2)}, u32[]{:S(2)}) collective-permute-start(bf16[2400,2400]{1,0:T(8,128)(2,1)} %param.6), channel_id=1, source_target_pairs={{0,1},{1,0},{2,3},{3,2},{4,5},{5,4},{6,7},{7,6},{8,9},{9,8},{10,11... | collective-permute-start | bytes 34560008 | tf_op jit(solution)/shard_map/ppermute | solution.py:101
  1.6 16.0 %collective-permute-start.2 = (bf16[10,8,640]{2,1,0:T(8,128)(2,1)S(1)}, bf16[10,8,640]{2,1,0:T(8,128)(2,1)S(1)}, u32[]{:S(2)}, u32[]{:S(2)}) collective-permute-start(bf16[10,8,640]{2,1,0:T(8,128)(2,1)S(1)} %get-tuple-element.28), channel_id=1, source_target_pairs={{0,2},{1,0},{2,6},{3,4},{4,3},{5,1},{6,7},{7,5},{8,10},{9,8},{10,1... | collective-permute-start | bytes 307208 | tf_op jit(solution)/shard_map/ppermute | solution.py:115
  4.2 13.4 %collective-permute-start.3 = (bf16[10,8,640]{2,1,0:T(8,128)(2,1)S(1)}, bf16[10,8,640]{2,1,0:T(8,128)(2,1)S(1)}, u32[]{:S(2)}, u32[]{:S(2)}) collective-permute-start(bf16[10,8,640]{2,1,0:T(8,128)(2,1)S(1)} %get-tuple-element.29), channel_id=1, source_target_pairs={{0,0},{1,2},{2,4},{3,6},{4,1},{5,3},{6,5},{7,7},{8,8},{9,10},{10,1... | collective-permute-start | bytes 307208 | tf_op jit(solution)/shard_map/ppermute | solution.py:115
  4.9 12.7 %collective-permute-start.1 = (bf16[10,8,640]{2,1,0:T(8,128)(2,1)S(1)}, bf16[10,8,640]{2,1,0:T(8,128)(2,1)S(1)}, u32[]{:S(2)}, u32[]{:S(2)}) collective-permute-start(bf16[10,8,640]{2,1,0:T(8,128)(2,1)S(1)} %get-tuple-element.30), channel_id=1, source_target_pairs={{0,4},{1,6},{2,0},{3,2},{4,5},{5,7},{6,1},{7,3},{8,12},{9,14},{10,... | collective-permute-start | bytes 307208 | tf_op jit(solution)/shard_map/ppermute | solution.py:115
  7.7 9.8 %collective-permute-start = (bf16[10,8,640]{2,1,0:T(8,128)(2,1)S(1)}, bf16[10,8,640]{2,1,0:T(8,128)(2,1)S(1)}, u32[]{:S(2)}, u32[]{:S(2)}) collective-permute-start(bf16[10,8,640]{2,1,0:T(8,128)(2,1)S(1)} %get-tuple-element.31), channel_id=1, source_target_pairs={{0,6},{1,4},{2,2},{3,0},{4,7},{5,5},{6,3},{7,1},{8,14},{9,12},{10,... | collective-permute-start | bytes 307208 | tf_op jit(solution)/shard_map/ppermute | solution.py:115
  17.8 21.5 %copy-start.1 = (bf16[5,8,8,640]{3,1,2,0:T(8,128)(2,1)}, bf16[5,8,8,640]{3,1,2,0:T(8,128)(2,1)S(1)}, u32[]{:S(2)}) copy-start(bf16[5,8,8,640]{3,1,2,0:T(8,128)(2,1)S(1)} %copy.4) | copy-start | bytes 1228804
  17.8 11.6 %collective-permute-start.5 = (bf16[40,5120]{1,0:T(8,128)(2,1)S(1)}, bf16[40,5120]{1,0:T(8,128)(2,1)S(1)}, u32[]{:S(2)}, u32[]{:S(2)}) collective-permute-start(bf16[40,5120]{1,0:T(8,128)(2,1)S(1)} %bitcast.24), channel_id=1, source_target_pairs={{0,16},{8,24},{16,0},{24,8},{1,17},{9,25},{17,1},{25,9},{2,18},{10... | collective-permute-start | bytes 1228808 | tf_op jit(solution)/shard_map/ppermute | solution.py:101
  18.2 11.7 %collective-permute-start.4 = (bf16[40,5120]{1,0:T(8,128)(2,1)S(1)}, bf16[40,5120]{1,0:T(8,128)(2,1)S(1)}, u32[]{:S(2)}, u32[]{:S(2)}) collective-permute-start(bf16[40,5120]{1,0:T(8,128)(2,1)S(1)} %bitcast.25), channel_id=1, source_target_pairs={{0,8},{8,0},{16,24},{24,16},{1,9},{9,1},{17,25},{25,17},{2,10},{10... | collective-permute-start | bytes 1228808 | tf_op jit(solution)/shard_map/ppermute | solution.py:101
  29.4 9.9 %copy-start.2 = (bf16[40,5120]{1,0:T(8,128)(2,1)}, bf16[40,5120]{1,0:T(8,128)(2,1)S(1)}, u32[]{:S(2)}) copy-start(bf16[40,5120]{1,0:T(8,128)(2,1)S(1)} %collective-permute-done.5.refs_3_) | copy-start | bytes 1228804
  29.4 6.4 %collective-permute-start.7 = (bf16[40,2560]{1,0:T(8,128)(2,1)S(1)}, bf16[40,2560]{1,0:T(8,128)(2,1)S(1)}, u32[]{:S(2)}, u32[]{:S(2)}) collective-permute-start(bf16[40,2560]{1,0:T(8,128)(2,1)S(1)} %slice.37), channel_id=1, source_target_pairs={{0,8},{8,0},{16,24},{24,16},{1,9},{9,1},{17,25},{25,17},{2,10},{10... | collective-permute-start | bytes 614408 | tf_op jit(solution)/shard_map/ppermute | solution.py:101
  29.9 9.4 %copy-start.3 = (bf16[40,5120]{1,0:T(8,128)(2,1)}, bf16[40,5120]{1,0:T(8,128)(2,1)S(1)}, u32[]{:S(2)}) copy-start(bf16[40,5120]{1,0:T(8,128)(2,1)S(1)} %collective-permute-done.4.refs_2_) | copy-start | bytes 1228804
  30.0 6.3 %collective-permute-start.6 = (bf16[40,2560]{1,0:T(8,128)(2,1)S(1)}, bf16[40,2560]{1,0:T(8,128)(2,1)S(1)}, u32[]{:S(2)}, u32[]{:S(2)}) collective-permute-start(bf16[40,2560]{1,0:T(8,128)(2,1)S(1)} %slice.36), channel_id=1, source_target_pairs={{0,16},{8,24},{16,0},{24,8},{1,17},{9,25},{17,1},{25,9},{2,18},{10... | collective-permute-start | bytes 614408 | tf_op jit(solution)/shard_map/ppermute | solution.py:101
  59.2 12.2 %collective-permute-start.11 = (s16[40,2432]{1,0:T(8,128)(2,1)S(1)}, s16[40,2432]{1,0:T(8,128)(2,1)S(1)}, u32[]{:S(2)}, u32[]{:S(2)}) collective-permute-start(s16[40,2432]{1,0:T(8,128)(2,1)S(1)} %get-tuple-element.21), channel_id=1, source_target_pairs={{0,6},{1,7},{2,4},{3,5},{4,2},{5,3},{6,0},{7,1},{8,14},{9,15},{10,... | collective-permute-start | bytes 583688 | tf_op jit(solution)/shard_map/ppermute | solution.py:101
  65.7 14.8 %collective-permute-start.10 = (s16[40,2432]{1,0:T(8,128)(2,1)S(1)}, s16[40,2432]{1,0:T(8,128)(2,1)S(1)}, u32[]{:S(2)}, u32[]{:S(2)}) collective-permute-start(s16[40,2432]{1,0:T(8,128)(2,1)S(1)} %get-tuple-element.22), channel_id=1, source_target_pairs={{0,4},{1,5},{2,6},{3,7},{4,0},{5,1},{6,2},{7,3},{8,12},{9,13},{10,... | collective-permute-start | bytes 583688 | tf_op jit(solution)/shard_map/ppermute | solution.py:101
  65.7 14.8 %collective-permute-start.9 = (s16[40,2432]{1,0:T(8,128)(2,1)S(1)}, s16[40,2432]{1,0:T(8,128)(2,1)S(1)}, u32[]{:S(2)}, u32[]{:S(2)}) collective-permute-start(s16[40,2432]{1,0:T(8,128)(2,1)S(1)} %get-tuple-element.23), channel_id=1, source_target_pairs={{0,2},{1,3},{2,0},{3,1},{4,6},{5,7},{6,4},{7,5},{8,10},{9,11},{10,... | collective-permute-start | bytes 583688 | tf_op jit(solution)/shard_map/ppermute | solution.py:101
  80.6 1.0 %copy-start = (f32[40,2400]{1,0:T(8,128)S(1)}, f32[40,2400]{1,0:T(8,128)}, u32[]{:S(2)}) copy-start(f32[40,2400]{1,0:T(8,128)} %get-tuple-element.19.refs_0_) | copy-start | bytes 1152004

commit v2 on v0

v2 whole, which is shorter than its diff:
```python
import jax
import jax.numpy as jnp
from jax import lax
from jax.experimental import pallas as pl
from jax.experimental.pallas import tpu as pltpu
from jax.sharding import PartitionSpec as P

LANES = 128
TILE_N = 512
QMAX = 32000.0
STEPS = 8.0
VMEM = pl.BlockSpec(memory_space=pltpu.VMEM)
SMEM = pl.BlockSpec(memory_space=pltpu.SMEM)


def round_up(value, unit):
    return -(-value // unit) * unit


def mask_kernel(base, where_ref, irreps_ref, row_ref, v_ref, out_ref, labels, held_left, held_right, sems):
    nv, width = v_ref.shape[1:]
    count, depth, padded = out_ref.shape
    middle = round_up(width // 2, LANES)
    spans = [(c, low, high) for c in range(count) for low, high in ((0, middle), (middle, width))]

    def fetch(i):
        c, low, high = spans[i]
        return pltpu.make_async_copy(v_ref.at[base + c, :, low:high], held(i).at[c], sems.at[i])

    def held(i):
        return held_left if i % 2 == 0 else held_right

    for i in range(len(spans)):
        fetch(i).start()
    row = row_ref[...]
    wide = jnp.concatenate([row, jnp.zeros((1, depth - nv), jnp.int32)], axis=1)
    labels[...] = jnp.broadcast_to(wide, (LANES, depth)).T
    first_a = where_ref[1]
    columns = jnp.concatenate([jnp.bitwise_xor(row, irreps_ref[first_a + a]) for a in range(width // nv)], axis=1)
    columns = columns.astype(jnp.bfloat16)
    for i, (c, low, high) in enumerate(spans):
        rows = jnp.bitwise_xor(labels[0:nv, :], irreps_ref[where_ref[0] + c]).astype(jnp.bfloat16)
        if low == 0:
            out_ref[c, nv:depth, :] = jnp.zeros((depth - nv, padded), jnp.bfloat16)
        fetch(i).wait()
        for n in range(low, high, LANES):
            end = min(n + LANES, high)
            keep = rows[:, 0:end - n] == columns[:, n:end]
            block = jnp.where(keep, held(i)[c, :, n - low:end - low], jnp.zeros((), jnp.bfloat16))
            if end < n + LANES:
                block = jnp.concatenate([block, jnp.zeros((nv, n + LANES - end), jnp.bfloat16)], axis=1)
            out_ref[c, 0:nv, n:n + LANES] = block


def dot_kernel(grp_count, where_ref, *refs):
    lhs_refs, part_refs = refs[:grp_count], refs[grp_count:-3]
    out_ref, wide, lhs = refs[-3:]
    group, chip = where_ref[0], where_ref[1]
    rows_each = lhs_refs[0].shape[0]
    per_group = where_ref.shape[0] - 2
    block = rows_each // per_group
    for j in range(grp_count):
        for q in range(per_group):
            at = jnp.bitwise_xor(jnp.bitwise_xor(group, j) * per_group + q, chip)
            rows = lhs_refs[j][q * block:(q + 1) * block, :].astype(jnp.float32)
            wide[pl.ds(pl.multiple_of(at * block, 8), block), :] = rows
    lhs[...] = wide[...].astype(jnp.bfloat16)
    padded = out_ref.shape[1]
    size = part_refs[0].shape[0] * part_refs[0].shape[1]
    for first in range(0, padded, TILE_N):
        last = min(first + TILE_N, padded)
        total = None
        for i, part_ref in enumerate(part_refs):
            right = part_ref[:, :, first:last].reshape(size, last - first)
            term = jnp.dot(lhs[:, i * size:(i + 1) * size], right, preferred_element_type=jnp.float32)
            total = term if total is None else total + term
        out_ref[:, first:last] = total


def code_kernel(width, mine_ref, theirs_ref, own_ref, *code_refs):
    count, padded = mine_ref.shape
    block = own_ref.shape[0]
    lane = lax.broadcasted_iota(jnp.int32, (count, LANES), 1)
    spare = width % LANES
    exponents = jnp.zeros((count, LANES), jnp.float32)
    for n in range(0, padded, LANES):
        part = mine_ref[:, n:n + LANES] + theirs_ref[:, n:n + LANES]
        own_ref[:, n:n + LANES] = part[:block]
        top = jnp.maximum(jnp.max(jnp.abs(part), axis=1, keepdims=True), 1e-30)
        level = jnp.ceil(jnp.log2(top) * STEPS + 0.05)
        code = jnp.round(part * (jnp.exp2(level * (-1.0 / STEPS)) * QMAX))
        exponents = jnp.where(lane == spare + n // LANES, level, exponents)
        if n + LANES == padded:
            code = jnp.where(lane >= spare, exponents, code)
        code = code.astype(jnp.int16)
        for r, code_ref in enumerate(code_refs, 1):
            code_ref[:, n:n + LANES] = code[r * block:(r + 1) * block]


def combine_kernel(width, own_ref, *refs):
    code_refs, out_ref = refs[:-1], refs[-1]
    base = width // LANES * LANES
    exponents = [jnp.exp2(ref[:, base:base + LANES].astype(jnp.float32) * (1.0 / STEPS)) * (1.0 / QMAX) for ref in code_refs]
    for low in range(0, width, LANES):
        high = min(low + LANES, width)
        at = width % LANES + low // LANES
        value = own_ref[:, low:high]
        for scale, ref in zip(exponents, code_refs):
            value = value + ref[:, low:high].astype(jnp.float32) * scale[:, at:at + 1]
        out_ref[:, low:high] = value


def shards(t_amps, vvvv, irreps):
    mem_count = lax.axis_size("mem")
    grp_count = lax.axis_size("grp")
    per_device, cw, nv = t_amps.shape
    chips = mem_count // 2
    cc = cw // chips
    half = cc // 2
    width = vvvv.shape[1]
    padded = round_up(width, LANES)
    depth = round_up(nv, LANES)
    a_local = width // nv
    mem = lax.axis_index("mem")
    group = lax.axis_index("grp")
    chip, core = mem // 2, mem % 2

    def swap(x, axis, k, count):
        return lax.ppermute(x, axis, [(i, i ^ k) for i in range(count)])

    hop = grp_count // 2

    def mask(source, owner, base, count):
        where = jnp.stack([owner * half + base, group * a_local]).astype(jnp.int32)
        blocks = pltpu.with_memory_space_constraint(source.reshape(half, nv, width), pltpu.HBM)
        return pl.pallas_call(
            lambda *refs: mask_kernel(base, *refs),
            in_specs=[SMEM, SMEM, VMEM, pl.BlockSpec(memory_space=pl.ANY)],
            out_specs=VMEM,
            out_shape=jax.ShapeDtypeStruct((count, depth, padded), jnp.bfloat16),
            scratch_shapes=[
                pltpu.VMEM((depth, LANES), jnp.int32),
                pltpu.VMEM((count, nv, round_up(width // 2, LANES)), jnp.bfloat16),
                pltpu.VMEM((count, nv, width - round_up(width // 2, LANES)), jnp.bfloat16),
                pltpu.SemaphoreType.DMA((2 * count,)),
            ],
            compiler_params=pltpu.CompilerParams(vmem_limit_bytes=16 * 2**20),
            cost_estimate=pl.CostEstimate(flops=0, bytes_accessed=4 * count * nv * width, transcendentals=0),
        )(where, irreps, irreps.reshape(1, nv), blocks)

    split = half // 2
    raw = t_amps.reshape(per_device, chips, 2, half, nv)
    kept = lax.dynamic_index_in_dim(raw, core, 2, keepdims=False)
    lent = swap(lax.dynamic_index_in_dim(raw, 1 - core, 2, keepdims=False), "mem", 1, mem_count)
    even = core == 0
    both = jnp.concatenate([jnp.where(even, kept, lent), jnp.where(even, lent, kept)])
    taken = [lax.dynamic_index_in_dim(both, jnp.bitwise_xor(chip, r), 1, keepdims=False) for r in range(chips)]
    got = [taken[0]] + [swap(taken[r], "mem", 2 * r, mem_count) for r in range(1, chips)]

    def beside(x):
        return [swap(x, "grp", 1, grp_count), swap(x, "grp", 2, grp_count)]

    def corner(near, far):
        cut = near.shape[0] // 2
        return jnp.concatenate([swap(near[:cut], "grp", 2, grp_count), swap(far[cut:], "grp", 1, grp_count)])

    x = jnp.concatenate(got[:chips // 2])
    y = jnp.concatenate(got[chips // 2:])
    x, late = lax.optimization_barrier((x, vvvv))
    x_beside = beside(x)
    parts = [mask(late, mem, 0, half)]
    x_beside, parts = lax.optimization_barrier((x_beside, parts))
    x_corner = corner(*x_beside)
    y_beside = beside(y)
    halves = [[x] + x_beside + [x_corner], [y] + y_beside + [corner(*y_beside)]]

    pair_rows = 2 * per_device
    kept_lhs, lent_lhs = [], []
    for one, two in zip(*halves):
        stack = jnp.concatenate([one, two]).reshape(chips, pair_rows, half, nv)
        stack = [stack[j] for j in range(chips)]
        bit = 1
        while bit < chips:
            flip = jnp.bitwise_and(chip, bit) != 0
            stack = [jnp.where(flip, stack[j ^ bit], stack[j]) for j in range(chips)]
            bit *= 2
        for lhs, target in ((kept_lhs, core), (lent_lhs, 1 - core)):
            first = target == 0
            rows = [jnp.where(first, stack[j], stack[j + hop]) for j in range(chips) if j // hop % 2 == 0]
            filled = jnp.pad(jnp.concatenate(rows), ((0, 0), (0, 0), (0, depth - nv)))
            lhs.append(filled.reshape(chips // 2 * pair_rows, half * depth))

    rows = grp_count * chips // 2 * pair_rows
    block = hop * pair_rows
    where = jnp.stack([group, chip] + [0] * (chips // grp_count)).astype(jnp.int32)

    def multiply(lhs):
        return pl.pallas_call(
            lambda *refs: dot_kernel(grp_count, *refs),
            in_specs=[SMEM] + [VMEM] * (grp_count + len(parts)),
            out_specs=VMEM,
            out_shape=jax.ShapeDtypeStruct((rows, padded), jnp.float32),
            scratch_shapes=[
                pltpu.VMEM((rows, half * depth), jnp.float32),
                pltpu.VMEM((rows, half * depth), jnp.bfloat16),
            ],
            compiler_params=pltpu.CompilerParams(vmem_limit_bytes=round_up(rows * half * depth * 6, 2**20) + 6 * 2**20),
            cost_estimate=pl.CostEstimate(flops=2 * rows * half * nv * width, bytes_accessed=4 * rows * width, transcendentals=0),
        )(where, *lhs, *parts)

    theirs = swap(multiply(lent_lhs), "mem", 1, mem_count)
    outs = pl.pallas_call(
        lambda *refs: code_kernel(width, *refs),
        in_specs=[VMEM] * 2,
        out_specs=[VMEM] * chips,
        out_shape=[jax.ShapeDtypeStruct((block, padded), jnp.float32)]
        + [jax.ShapeDtypeStruct((block, padded), jnp.int16)] * (chips - 1),
        compiler_params=pltpu.CompilerParams(vmem_limit_bytes=16 * 2**20),
    )(multiply(kept_lhs), theirs)

    arrived = [swap(outs[r], "mem", 2 * r, mem_count) for r in range(1, chips)]
    return pl.pallas_call(
        lambda *refs: combine_kernel(width, *refs),
        out_shape=jax.ShapeDtypeStruct((block, width), jnp.float32),
        compiler_params=pltpu.CompilerParams(vmem_limit_bytes=8 * 2**20),
    )(outs[0], *arrived)


def solution(mesh):
    in_specs = (P(("grp", "mem"), None, None), P("mem", "grp"), P())
    out_specs = P("mem", "grp")
    return jax.shard_map(shards, mesh=mesh, in_specs=in_specs, out_specs=out_specs, check_vma=False)
```

time: 125 us -> 63.7 us (0.51)
  the two profiles are of different devices: /device:TPU:0 before, /device:TPU:8 now
where the time goes in v2:
time: 63.7 us; the launch traced here: 63.5 us
  waiting for transfers between devices  26.2 us (41%)
  starting transfers between devices  18.9 us (30%)
  Pallas kernels  13.2 us (21%)
  other arithmetic  2.68 us (4%)
  local copies, waits for them, and re-layouts  2.14 us (3%)
    ppermute x16, waiting for transfers between devices, swap(): return lax.ppermute(x, axis, [(i, i ^ k) for i in range(count)])  26.2 us
    ppermute x16, starting transfers between devices, swap(): return lax.ppermute(x, axis, [(i, i ^ k) for i in range(count)])  18.9 us
    pallas_call x2, Pallas kernels, multiply(): pl.pallas_call(lambda *refs: dot_kernel(grp_count, *refs), in_specs=[SMEM...  6.03 us
    pallas_call x1, Pallas kernels, mask(): pl.pallas_call(lambda *refs: mask_kernel(base, *refs), in_specs=[SMEM, SM...  5.28 us
  transfers between devices with their start and end apart: 16, of which 11 were waited for; matrix products, arithmetic and copies ran while one was open for 4% of the time, Pallas kernels for 13%

profile of v2, /device:TPU:8, one launch (start us, length us, event | category | flops | bytes accessed | tf_op | source)
XLA Modules:
  0.0 63.5 jit_solution(11122017438575802503)
XLA Ops:
  0.0 1.1 %reshape.69 = bf16[10,4,2,4,600]{4,3,2,1,0:T(4,128)(2,1)S(1)} reshape(bf16[10,32,600]{2,1,0:T(8,128)(2,1)} %param.3) | data formatting | bytes 768000 | tf_op jit(solution)/shard_map/reshape | solution.py:152
  3.4 3.1 %collective-permute-start.1 = (bf16[20,4,600]{2,1,0:T(4,128)(2,1)S(1)}, bf16[20,4,600]{2,1,0:T(4,128)(2,1)S(1)}, u32[]{:S(2)}, u32[]{:S(2)}) collective-permute-start(bf16[20,4,600]{2,1,0:T(4,128)(2,1)S(1)} %get-tuple-element.40), channel_id=1, source_target_pairs={{0,6},{1,7},{2,4},{3,5},{4,2},{5,3},{6,0},{7,1},{8,14},{9,15},{10,... | collective-permute-start | bytes 288008 | tf_op jit(solution)/shard_map/ppermute | solution.py:129
  6.5 1.2 %collective-permute-start.2 = (bf16[20,4,600]{2,1,0:T(4,128)(2,1)S(1)}, bf16[20,4,600]{2,1,0:T(4,128)(2,1)S(1)}, u32[]{:S(2)}, u32[]{:S(2)}) collective-permute-start(bf16[20,4,600]{2,1,0:T(4,128)(2,1)S(1)} %get-tuple-element.41), channel_id=1, source_target_pairs={{0,4},{1,5},{2,6},{3,7},{4,0},{5,1},{6,2},{7,3},{8,12},{9,13},{10,... | collective-permute-start | bytes 288008 | tf_op jit(solution)/shard_map/ppermute | solution.py:129
  8.4 1.6 %collective-permute-start.5 = (bf16[40,4,600]{2,1,0:T(4,128)(2,1)S(1)}, bf16[40,4,600]{2,1,0:T(4,128)(2,1)S(1)}, u32[]{:S(2)}, u32[]{:S(2)}) collective-permute-start(bf16[40,4,600]{2,1,0:T(4,128)(2,1)S(1)} %pad_maximum_fusion), channel_id=1, source_target_pairs={{0,8},{8,0},{16,24},{24,16},{1,9},{9,1},{17,25},{25,17},{2,10},{10... | collective-permute-start | bytes 576008 | tf_op jit(solution)/shard_map/ppermute | solution.py:129
  9.9 1.5 %collective-permute-start.6 = (bf16[40,4,600]{2,1,0:T(4,128)(2,1)S(1)}, bf16[40,4,600]{2,1,0:T(4,128)(2,1)S(1)}, u32[]{:S(2)}, u32[]{:S(2)}) collective-permute-start(bf16[40,4,600]{2,1,0:T(4,128)(2,1)S(1)} %pad_maximum_fusion), channel_id=1, source_target_pairs={{0,16},{8,24},{16,0},{24,8},{1,17},{9,25},{17,1},{25,9},{2,18},{10... | collective-permute-start | bytes 576008 | tf_op jit(solution)/shard_map/ppermute | solution.py:129
  11.4 2.8 %collective-permute-done.1 = bf16[20,4,600]{2,1,0:T(4,128)(2,1)S(1)} collective-permute-done((bf16[20,4,600]{2,1,0:T(4,128)(2,1)S(1)}, bf16[20,4,600]{2,1,0:T(4,128)(2,1)S(1)}, u32[]{:S(2)}, u32[]{:S(2)}) %collective-permute-start.1) | collective-permute-done | bytes 96032 | tf_op jit(solution)/shard_map/ppermute | solution.py:129
  14.2 1.0 %collective-permute-done.2 = bf16[20,4,600]{2,1,0:T(4,128)(2,1)S(1)} collective-permute-done((bf16[20,4,600]{2,1,0:T(4,128)(2,1)S(1)}, bf16[20,4,600]{2,1,0:T(4,128)(2,1)S(1)}, u32[]{:S(2)}, u32[]{:S(2)}) %collective-permute-start.2) | collective-permute-done | bytes 96032 | tf_op jit(solution)/shard_map/ppermute | solution.py:129
  15.6 1.6 %collective-permute-start.7 = (bf16[40,4,600]{2,1,0:T(4,128)(2,1)S(1)}, bf16[40,4,600]{2,1,0:T(4,128)(2,1)S(1)}, u32[]{:S(2)}, u32[]{:S(2)}) collective-permute-start(bf16[40,4,600]{2,1,0:T(4,128)(2,1)S(1)} %constant_dynamic-update-slice_fusion), channel_id=1, source_target_pairs={{0,16},{8,24},{16,0},{24,8},{1,17},{9,25},{17,1},{25,9},{2,18},{10... | collective-permute-start | bytes 576008 | tf_op jit(solution)/shard_map/ppermute | solution.py:129
  17.3 1.5 %collective-permute-start.4 = (bf16[40,4,600]{2,1,0:T(4,128)(2,1)S(1)}, bf16[40,4,600]{2,1,0:T(4,128)(2,1)S(1)}, u32[]{:S(2)}, u32[]{:S(2)}) collective-permute-start(bf16[40,4,600]{2,1,0:T(4,128)(2,1)S(1)} %constant_dynamic-update-slice_fusion), channel_id=1, source_target_pairs={{0,8},{8,0},{16,24},{24,16},{1,9},{9,1},{17,25},{25,17},{2,10},{10... | collective-permute-start | bytes 576008 | tf_op jit(solution)/shard_map/ppermute | solution.py:129
  19.0 5.3 %shard_map.37.refs_5_ = bf16[4,640,2432]{2,1,0:T(8,128)(2,1)S(1)} custom-call(s32[2]{0:T(128)S(1)} %pad_add_fusion.1.refs_0_, s32[600]{0:T(1024)S(1)} %copy-done, s32[1,600]{1,0:T(1,128)S(1)} %reshape.71.refs_2_, bf16[4,600,2400]{2,1,0:T(8,128)(2,1)} %bitcast.54), custom_call_target="tpu_custom_call" | custom-call | bytes 23040000 | tf_op jit(solution)/shard_map/pallas_call | solution.py:136
  25.7 1.5 %collective-permute-start.9 = (bf16[20,4,600]{2,1,0:T(4,128)(2,1)S(1)}, bf16[20,4,600]{2,1,0:T(4,128)(2,1)S(1)}, u32[]{:S(2)}, u32[]{:S(2)}) collective-permute-start(bf16[20,4,600]{2,1,0:T(4,128)(2,1)S(1)} %get-tuple-element.46), channel_id=1, source_target_pairs={{0,16},{8,24},{16,0},{24,8},{1,17},{9,25},{17,1},{25,9},{2,18},{10... | collective-permute-start | bytes 288008 | tf_op jit(solution)/shard_map/ppermute | solution.py:129
  27.7 1.5 %collective-permute-start.8 = (bf16[20,4,600]{2,1,0:T(4,128)(2,1)S(1)}, bf16[20,4,600]{2,1,0:T(4,128)(2,1)S(1)}, u32[]{:S(2)}, u32[]{:S(2)}) collective-permute-start(bf16[20,4,600]{2,1,0:T(4,128)(2,1)S(1)} %get-tuple-element.44), channel_id=1, source_target_pairs={{0,8},{8,0},{16,24},{24,16},{1,9},{9,1},{17,25},{25,17},{2,10},{10... | collective-permute-start | bytes 288008 | tf_op jit(solution)/shard_map/ppermute | solution.py:129
  29.8 1.1 %collective-permute-done.9 = bf16[20,4,600]{2,1,0:T(4,128)(2,1)S(1)} collective-permute-done((bf16[20,4,600]{2,1,0:T(4,128)(2,1)S(1)}, bf16[20,4,600]{2,1,0:T(4,128)(2,1)S(1)}, u32[]{:S(2)}, u32[]{:S(2)}) %collective-permute-start.9) | collective-permute-done | bytes 96032 | tf_op jit(solution)/shard_map/ppermute | solution.py:129
  30.9 0.9 %collective-permute-done.10 = bf16[20,4,600]{2,1,0:T(4,128)(2,1)S(1)} collective-permute-done((bf16[20,4,600]{2,1,0:T(4,128)(2,1)S(1)}, bf16[20,4,600]{2,1,0:T(4,128)(2,1)S(1)}, u32[]{:S(2)}, u32[]{:S(2)}) %collective-permute-start.10) | collective-permute-done | bytes 96032 | tf_op jit(solution)/shard_map/ppermute | solution.py:129
  31.9 1.1 %collective-permute-done.8 = bf16[20,4,600]{2,1,0:T(4,128)(2,1)S(1)} collective-permute-done((bf16[20,4,600]{2,1,0:T(4,128)(2,1)S(1)}, bf16[20,4,600]{2,1,0:T(4,128)(2,1)S(1)}, u32[]{:S(2)}, u32[]{:S(2)}) %collective-permute-start.8) | collective-permute-done | bytes 96032 | tf_op jit(solution)/shard_map/ppermute | solution.py:129
  33.3 3.0 %shard_map.39 = f32[160,2432]{1,0:T(8,128)S(1)} custom-call(s32[3]{0:T(128)S(1)} %pad_add_fusion.refs_0_, bf16[40,2560]{1,0:T(8,128)(2,1)S(1)} %bitcast.46, bf16[40,2560]{1,0:T(8,128)(2,1)S(1)} %bitcast.48, bf16[40,2560]{1,0:T(8,128)(2,1)S(1)} %bitcast.47, bf16[40,2560]{1,0:T(8,128)(2,1)S(1)} %bitcast.53, bf16[4,640,2432]{2,1,0:T(8,128)(2,1)S(1)} %shard_map.37.refs_5_), custom_call_target="tpu_custom_call" | custom-call | flops 1843200000 | bytes 1536000 | tf_op jit(solution)/shard_map/pallas_call | solution.py:198
  36.7 3.0 %shard_map.38.refs_0_ = f32[160,2432]{1,0:T(8,128)S(1)} custom-call(s32[3]{0:T(128)S(1)} %pad_add_fusion.refs_0_, bf16[40,2560]{1,0:T(8,128)(2,1)S(1)} %bitcast.49, bf16[40,2560]{1,0:T(8,128)(2,1)S(1)} %bitcast.50, bf16[40,2560]{1,0:T(8,128)(2,1)S(1)} %bitcast.51, bf16[40,2560]{1,0:T(8,128)(2,1)S(1)} %bitcast.52, bf16[4,640,2432]{2,1,0:T(8,128)(2,1)S(1)} %shard_map.37.refs_5_), custom_call_target="tpu_custom_call" | custom-call | flops 1843200000 | bytes 1536000 | tf_op jit(solution)/shard_map/pallas_call | solution.py:198
  39.8 0.8 %shard_map.40 = (f32[40,2432]{1,0:T(8,128)S(1)}, s16[40,2432]{1,0:T(8,128)(2,1)S(1)}, s16[40,2432]{1,0:T(8,128)(2,1)S(1)}, s16[40,2432]{1,0:T(8,128)(2,1)S(1)}) custom-call(f32[160,2432]{1,0:T(8,128)S(1)} %shard_map.38.refs_0_, f32[160,2432]{1,0:T(8,128)S(1)} %collective-permute-done.12.refs_1_), custom_call_target="tpu_custom_call" | custom-call | tf_op jit(solution)/shard_map/pallas_call | solution.py:212
  40.5 2.3 %collective-permute-start.13 = (s16[40,2432]{1,0:T(8,128)(2,1)S(1)}, s16[40,2432]{1,0:T(8,128)(2,1)S(1)}, u32[]{:S(2)}, u32[]{:S(2)}) collective-permute-start(s16[40,2432]{1,0:T(8,128)(2,1)S(1)} %get-tuple-element.20), channel_id=1, source_target_pairs={{0,2},{1,3},{2,0},{3,1},{4,6},{5,7},{6,4},{7,5},{8,10},{9,11},{10,... | collective-permute-start | bytes 583688 | tf_op jit(solution)/shard_map/ppermute | solution.py:129
  42.8 1.3 %collective-permute-start.14 = (s16[40,2432]{1,0:T(8,128)(2,1)S(1)}, s16[40,2432]{1,0:T(8,128)(2,1)S(1)}, u32[]{:S(2)}, u32[]{:S(2)}) collective-permute-start(s16[40,2432]{1,0:T(8,128)(2,1)S(1)} %get-tuple-element.21), channel_id=1, source_target_pairs={{0,4},{1,5},{2,6},{3,7},{4,0},{5,1},{6,2},{7,3},{8,12},{9,13},{10,... | collective-permute-start | bytes 583688 | tf_op jit(solution)/shard_map/ppermute | solution.py:129
  44.6 6.9 %collective-permute-done.13.refs_1_ = s16[40,2432]{1,0:T(8,128)(2,1)S(1)} collective-permute-done((s16[40,2432]{1,0:T(8,128)(2,1)S(1)}, s16[40,2432]{1,0:T(8,128)(2,1)S(1)}, u32[]{:S(2)}, u32[]{:S(2)}) %collective-permute-start.13) | collective-permute-done | bytes 194592 | tf_op jit(solution)/shard_map/ppermute | solution.py:129
  51.4 6.2 %collective-permute-done.14.refs_2_ = s16[40,2432]{1,0:T(8,128)(2,1)S(1)} collective-permute-done((s16[40,2432]{1,0:T(8,128)(2,1)S(1)}, s16[40,2432]{1,0:T(8,128)(2,1)S(1)}, u32[]{:S(2)}, u32[]{:S(2)}) %collective-permute-start.14) | collective-permute-done | bytes 194592 | tf_op jit(solution)/shard_map/ppermute | solution.py:129
  57.6 4.7 %collective-permute-done.15.refs_3_ = s16[40,2432]{1,0:T(8,128)(2,1)S(1)} collective-permute-done((s16[40,2432]{1,0:T(8,128)(2,1)S(1)}, s16[40,2432]{1,0:T(8,128)(2,1)S(1)}, u32[]{:S(2)}, u32[]{:S(2)}) %collective-permute-start.15) | collective-permute-done | bytes 194592 | tf_op jit(solution)/shard_map/ppermute | solution.py:129
  62.3 1.2 %shard_map.41 = f32[40,2400]{1,0:T(8,128)} custom-call(f32[40,2432]{1,0:T(8,128)S(1)} %get-tuple-element.19.refs_0_, s16[40,2432]{1,0:T(8,128)(2,1)S(1)} %collective-permute-done.13.refs_1_, s16[40,2432]{1,0:T(8,128)(2,1)S(1)} %collective-permute-done.14.refs_2_, s16[40,2432]{1,0:T(8,128)(2,1)S(1)} %collective-permute-done.15.refs_3_), custom_call_target="tpu_custom_call" | custom-call | tf_op jit(solution)/shard_map/pallas_call | solution.py:222
  (44 shorter events, 7.0 us)
Async XLA Ops:
  1.2 1.5 %collective-permute-start = (bf16[10,4,4,600]{3,2,1,0:T(4,128)(2,1)S(1)}, bf16[10,4,4,600]{3,2,1,0:T(4,128)(2,1)S(1)}, u32[]{:S(2)}, u32[]{:S(2)}) collective-permute-start(bf16[10,4,4,600]{3,2,1,0:T(4,128)(2,1)S(1)} %dynamic-slice_bitcast_fusion), channel_id=1, source_target_pairs={{0,1},{1,0},{2,3},{3,2},{4,5},{5,4},{6,7},{7,6},{8,9},{9,8},{10,11... | collective-permute-start | bytes 576008 | tf_op jit(solution)/shard_map/ppermute | solution.py:129
  3.2 15.8 %copy-start = (s32[600]{0:T(1024)S(1)}, s32[600]{0:T(1024)}, u32[]{:S(2)}) copy-start(s32[600]{0:T(1024)} %refs_1_.1) | copy-start | bytes 7204
  3.2 5.0 %collective-permute-start.3 = (bf16[20,4,600]{2,1,0:T(4,128)(2,1)S(1)}, bf16[20,4,600]{2,1,0:T(4,128)(2,1)S(1)}, u32[]{:S(2)}, u32[]{:S(2)}) collective-permute-start(bf16[20,4,600]{2,1,0:T(4,128)(2,1)S(1)} %get-tuple-element.42), channel_id=1, source_target_pairs={{0,2},{1,3},{2,0},{3,1},{4,6},{5,7},{6,4},{7,5},{8,10},{9,11},{10,... | collective-permute-start | bytes 288008 | tf_op jit(solution)/shard_map/ppermute | solution.py:129
  3.4 10.8 %collective-permute-start.1 = (bf16[20,4,600]{2,1,0:T(4,128)(2,1)S(1)}, bf16[20,4,600]{2,1,0:T(4,128)(2,1)S(1)}, u32[]{:S(2)}, u32[]{:S(2)}) collective-permute-start(bf16[20,4,600]{2,1,0:T(4,128)(2,1)S(1)} %get-tuple-element.40), channel_id=1, source_target_pairs={{0,6},{1,7},{2,4},{3,5},{4,2},{5,3},{6,0},{7,1},{8,14},{9,15},{10,... | collective-permute-start | bytes 288008 | tf_op jit(solution)/shard_map/ppermute | solution.py:129
  6.5 8.7 %collective-permute-start.2 = (bf16[20,4,600]{2,1,0:T(4,128)(2,1)S(1)}, bf16[20,4,600]{2,1,0:T(4,128)(2,1)S(1)}, u32[]{:S(2)}, u32[]{:S(2)}) collective-permute-start(bf16[20,4,600]{2,1,0:T(4,128)(2,1)S(1)} %get-tuple-element.41), channel_id=1, source_target_pairs={{0,4},{1,5},{2,6},{3,7},{4,0},{5,1},{6,2},{7,3},{8,12},{9,13},{10,... | collective-permute-start | bytes 288008 | tf_op jit(solution)/shard_map/ppermute | solution.py:129
  8.4 15.9 %collective-permute-start.5 = (bf16[40,4,600]{2,1,0:T(4,128)(2,1)S(1)}, bf16[40,4,600]{2,1,0:T(4,128)(2,1)S(1)}, u32[]{:S(2)}, u32[]{:S(2)}) collective-permute-start(bf16[40,4,600]{2,1,0:T(4,128)(2,1)S(1)} %pad_maximum_fusion), channel_id=1, source_target_pairs={{0,8},{8,0},{16,24},{24,16},{1,9},{9,1},{17,25},{25,17},{2,10},{10... | collective-permute-start | bytes 576008 | tf_op jit(solution)/shard_map/ppermute | solution.py:129
  9.9 14.4 %collective-permute-start.6 = (bf16[40,4,600]{2,1,0:T(4,128)(2,1)S(1)}, bf16[40,4,600]{2,1,0:T(4,128)(2,1)S(1)}, u32[]{:S(2)}, u32[]{:S(2)}) collective-permute-start(bf16[40,4,600]{2,1,0:T(4,128)(2,1)S(1)} %pad_maximum_fusion), channel_id=1, source_target_pairs={{0,16},{8,24},{16,0},{24,8},{1,17},{9,25},{17,1},{25,9},{2,18},{10... | collective-permute-start | bytes 576008 | tf_op jit(solution)/shard_map/ppermute | solution.py:129
  15.6 8.7 %collective-permute-start.7 = (bf16[40,4,600]{2,1,0:T(4,128)(2,1)S(1)}, bf16[40,4,600]{2,1,0:T(4,128)(2,1)S(1)}, u32[]{:S(2)}, u32[]{:S(2)}) collective-permute-start(bf16[40,4,600]{2,1,0:T(4,128)(2,1)S(1)} %constant_dynamic-update-slice_fusion), channel_id=1, source_target_pairs={{0,16},{8,24},{16,0},{24,8},{1,17},{9,25},{17,1},{25,9},{2,18},{10... | collective-permute-start | bytes 576008 | tf_op jit(solution)/shard_map/ppermute | solution.py:129
  17.3 7.6 %collective-permute-start.4 = (bf16[40,4,600]{2,1,0:T(4,128)(2,1)S(1)}, bf16[40,4,600]{2,1,0:T(4,128)(2,1)S(1)}, u32[]{:S(2)}, u32[]{:S(2)}) collective-permute-start(bf16[40,4,600]{2,1,0:T(4,128)(2,1)S(1)} %constant_dynamic-update-slice_fusion), channel_id=1, source_target_pairs={{0,8},{8,0},{16,24},{24,16},{1,9},{9,1},{17,25},{25,17},{2,10},{10... | collective-permute-start | bytes 576008 | tf_op jit(solution)/shard_map/ppermute | solution.py:129
  25.1 4.7 %collective-permute-start.11 = (bf16[20,4,600]{2,1,0:T(4,128)(2,1)S(1)}, bf16[20,4,600]{2,1,0:T(4,128)(2,1)S(1)}, u32[]{:S(2)}, u32[]{:S(2)}) collective-permute-start(bf16[20,4,600]{2,1,0:T(4,128)(2,1)S(1)} %get-tuple-element.45), channel_id=1, source_target_pairs={{0,16},{8,24},{16,0},{24,8},{1,17},{9,25},{17,1},{25,9},{2,18},{10... | collective-permute-start | bytes 288008 | tf_op jit(solution)/shard_map/ppermute | solution.py:129
  25.7 5.3 %collective-permute-start.9 = (bf16[20,4,600]{2,1,0:T(4,128)(2,1)S(1)}, bf16[20,4,600]{2,1,0:T(4,128)(2,1)S(1)}, u32[]{:S(2)}, u32[]{:S(2)}) collective-permute-start(bf16[20,4,600]{2,1,0:T(4,128)(2,1)S(1)} %get-tuple-element.46), channel_id=1, source_target_pairs={{0,16},{8,24},{16,0},{24,8},{1,17},{9,25},{17,1},{25,9},{2,18},{10... | collective-permute-start | bytes 288008 | tf_op jit(solution)/shard_map/ppermute | solution.py:129
  27.2 4.7 %collective-permute-start.10 = (bf16[20,4,600]{2,1,0:T(4,128)(2,1)S(1)}, bf16[20,4,600]{2,1,0:T(4,128)(2,1)S(1)}, u32[]{:S(2)}, u32[]{:S(2)}) collective-permute-start(bf16[20,4,600]{2,1,0:T(4,128)(2,1)S(1)} %get-tuple-element.43), channel_id=1, source_target_pairs={{0,8},{8,0},{16,24},{24,16},{1,9},{9,1},{17,25},{25,17},{2,10},{10... | collective-permute-start | bytes 288008 | tf_op jit(solution)/shard_map/ppermute | solution.py:129
  27.7 5.2 %collective-permute-start.8 = (bf16[20,4,600]{2,1,0:T(4,128)(2,1)S(1)}, bf16[20,4,600]{2,1,0:T(4,128)(2,1)S(1)}, u32[]{:S(2)}, u32[]{:S(2)}) collective-permute-start(bf16[20,4,600]{2,1,0:T(4,128)(2,1)S(1)} %get-tuple-element.44), channel_id=1, source_target_pairs={{0,8},{8,0},{16,24},{24,16},{1,9},{9,1},{17,25},{25,17},{2,10},{10... | collective-permute-start | bytes 288008 | tf_op jit(solution)/shard_map/ppermute | solution.py:129
  36.3 3.5 %collective-permute-start.12 = (f32[160,2432]{1,0:T(8,128)S(1)}, f32[160,2432]{1,0:T(8,128)S(1)}, u32[]{:S(2)}, u32[]{:S(2)}) collective-permute-start(f32[160,2432]{1,0:T(8,128)S(1)} %shard_map.39), channel_id=1, source_target_pairs={{0,1},{1,0},{2,3},{3,2},{4,5},{5,4},{6,7},{7,6},{8,9},{9,8},{10,11... | collective-permute-start | bytes 4669448 | tf_op jit(solution)/shard_map/ppermute | solution.py:129
  40.5 10.9 %collective-permute-start.13 = (s16[40,2432]{1,0:T(8,128)(2,1)S(1)}, s16[40,2432]{1,0:T(8,128)(2,1)S(1)}, u32[]{:S(2)}, u32[]{:S(2)}) collective-permute-start(s16[40,2432]{1,0:T(8,128)(2,1)S(1)} %get-tuple-element.20), channel_id=1, source_target_pairs={{0,2},{1,3},{2,0},{3,1},{4,6},{5,7},{6,4},{7,5},{8,10},{9,11},{10,... | collective-permute-start | bytes 583688 | tf_op jit(solution)/shard_map/ppermute | solution.py:129
  42.8 14.8 %collective-permute-start.14 = (s16[40,2432]{1,0:T(8,128)(2,1)S(1)}, s16[40,2432]{1,0:T(8,128)(2,1)S(1)}, u32[]{:S(2)}, u32[]{:S(2)}) collective-permute-start(s16[40,2432]{1,0:T(8,128)(2,1)S(1)} %get-tuple-element.21), channel_id=1, source_target_pairs={{0,4},{1,5},{2,6},{3,7},{4,0},{5,1},{6,2},{7,3},{8,12},{9,13},{10,... | collective-permute-start | bytes 583688 | tf_op jit(solution)/shard_map/ppermute | solution.py:129
  44.1 18.3 %collective-permute-start.15 = (s16[40,2432]{1,0:T(8,128)(2,1)S(1)}, s16[40,2432]{1,0:T(8,128)(2,1)S(1)}, u32[]{:S(2)}, u32[]{:S(2)}) collective-permute-start(s16[40,2432]{1,0:T(8,128)(2,1)S(1)} %get-tuple-element.22), channel_id=1, source_target_pairs={{0,6},{1,7},{2,4},{3,5},{4,2},{5,3},{6,0},{7,1},{8,14},{9,15},{10,... | collective-permute-start | bytes 583688 | tf_op jit(solution)/shard_map/ppermute | solution.py:129

commit v3 on v2

--- a/solution.py
+++ b/solution.py
@@ -77,36 +77,80 @@
         out_ref[:, first:last] = total
 
 
-def code_kernel(width, mine_ref, theirs_ref, own_ref, *code_refs):
+def encode(part, lane, at, exponents):
+    top = jnp.maximum(jnp.max(jnp.abs(part), axis=1, keepdims=True), 1e-30)
+    level = jnp.ceil(jnp.log2(top) * STEPS + 0.05)
+    code = jnp.round(part * (jnp.exp2(level * (-1.0 / STEPS)) * QMAX))
+    return code, jnp.where(lane == at, level, exponents)
+
+
+def scale_of(ref):
+    last = ref[:, ref.shape[1] - LANES:].astype(jnp.float32)
+    return jnp.exp2(last * (1.0 / STEPS)) * (1.0 / QMAX)
+
+
+def code_kernel(width, split, mine_ref, theirs_ref, own_ref, next_ref, *refs):
     count, padded = mine_ref.shape
     block = own_ref.shape[0]
+    chips = count // block
+    low_refs, high_refs = refs[:chips - 2], refs[chips - 2:]
     lane = lax.broadcasted_iota(jnp.int32, (count, LANES), 1)
     spare = width % LANES
     exponents = jnp.zeros((count, LANES), jnp.float32)
     for n in range(0, padded, LANES):
         part = mine_ref[:, n:n + LANES] + theirs_ref[:, n:n + LANES]
         own_ref[:, n:n + LANES] = part[:block]
-        top = jnp.maximum(jnp.max(jnp.abs(part), axis=1, keepdims=True), 1e-30)
-        level = jnp.ceil(jnp.log2(top) * STEPS + 0.05)
-        code = jnp.round(part * (jnp.exp2(level * (-1.0 / STEPS)) * QMAX))
-        exponents = jnp.where(lane == spare + n // LANES, level, exponents)
+        code, exponents = encode(part, lane, spare + n // LANES, exponents)
         if n + LANES == padded:
             code = jnp.where(lane >= spare, exponents, code)
         code = code.astype(jnp.int16)
-        for r, code_ref in enumerate(code_refs, 1):
-            code_ref[:, n:n + LANES] = code[r * block:(r + 1) * block]
-
-
-def combine_kernel(width, own_ref, *refs):
-    code_refs, out_ref = refs[:-1], refs[-1]
-    base = width // LANES * LANES
-    exponents = [jnp.exp2(ref[:, base:base + LANES].astype(jnp.float32) * (1.0 / STEPS)) * (1.0 / QMAX) for ref in code_refs]
+        next_ref[:, n:n + LANES] = code[block:2 * block]
+        for r in range(2, chips):
+            rows = slice(r * block, (r + 1) * block)
+            if n < split:
+                low_refs[r - 2][:, n:n + LANES] = code[rows]
+            elif r % 2 == 0:
+                high_refs[r - 2][:, n - split:n - split + LANES] = part[rows]
+            else:
+                high_refs[r - 2][:, n - split:n - split + LANES] = code[rows]
+    exponents = exponents.astype(jnp.int16)
+    for r in range(2, chips):
+        low_refs[r - 2][:, split:split + LANES] = exponents[r * block:(r + 1) * block]
+
+
+def relay_kernel(width, split, *refs):
+    count = len(refs) // 3
+    spare = width % LANES
+    for mine_ref, code_ref, out_ref in zip(refs[:count], refs[count:2 * count], refs[2 * count:]):
+        block, size = mine_ref.shape
+        lane = lax.broadcasted_iota(jnp.int32, (block, LANES), 1)
+        scale = scale_of(code_ref)
+        exponents = jnp.zeros((block, LANES), jnp.float32)
+        for n in range(0, size, LANES):
+            at = spare + (n + split) // LANES
+            part = mine_ref[:, n:n + LANES] + code_ref[:, n:n + LANES].astype(jnp.float32) * scale[:, at:at + 1]
+            if n + LANES == size:
+                part = jnp.where(lane < spare, part, 0.0)
+            code, exponents = encode(part, lane, at, exponents)
+            if n + LANES == size:
+                code = jnp.where(lane >= spare, exponents, code)
+            out_ref[:, n:n + LANES] = code.astype(jnp.int16)
+
+
+def combine_kernel(width, split, own_ref, next_ref, *refs):
+    out_ref = refs[-1]
+    cut = 2 * (len(refs) - 1) // 3
+    lows, highs = refs[:cut], refs[cut:-1]
+    next_scale = scale_of(next_ref)
+    low_scales = [scale_of(ref) for ref in lows]
+    high_scales = [scale_of(ref) for ref in highs]
     for low in range(0, width, LANES):
         high = min(low + LANES, width)
         at = width % LANES + low // LANES
-        value = own_ref[:, low:high]
-        for scale, ref in zip(exponents, code_refs):
-            value = value + ref[:, low:high].astype(jnp.float32) * scale[:, at:at + 1]
+        value = own_ref[:, low:high] + next_ref[:, low:high].astype(jnp.float32) * next_scale[:, at:at + 1]
+        some, scales, base = (lows, low_scales, 0) if low < split else (highs, high_scales, split)
+        for scale, ref in zip(scales, some):
+            value = value + ref[:, low - base:high - base].astype(jnp.float32) * scale[:, at:at + 1]
         out_ref[:, low:high] = value
 
 
@@ -164,15 +208,18 @@
         cut = near.shape[0] // 2
         return jnp.concatenate([swap(near[:cut], "grp", 2, grp_count), swap(far[cut:], "grp", 1, grp_count)])
 
+    def around(x):
+        return [x] + [swap(x, "grp", k, grp_count) for k in range(1, grp_count)]
+
     x = jnp.concatenate(got[:chips // 2])
     y = jnp.concatenate(got[chips // 2:])
-    x, late = lax.optimization_barrier((x, vvvv))
-    x_beside = beside(x)
-    parts = [mask(late, mem, 0, half)]
-    x_beside, parts = lax.optimization_barrier((x_beside, parts))
-    x_corner = corner(*x_beside)
-    y_beside = beside(y)
-    halves = [[x] + x_beside + [x_corner], [y] + y_beside + [corner(*y_beside)]]
+    x_all = around(x)
+    y, late = lax.optimization_barrier((y, vvvv))
+    parts = [mask(late, mem, 0, half // 2)]
+    x_all, parts, late = lax.optimization_barrier((x_all, parts, late))
+    y_all, part = lax.optimization_barrier((around(y), mask(late, mem, half // 2, half // 2)))
+    parts.append(part)
+    halves = [x_all, y_all]
 
     pair_rows = 2 * per_device
     kept_lhs, lent_lhs = [], []
@@ -209,21 +256,43 @@
         )(where, *lhs, *parts)
 
     theirs = swap(multiply(lent_lhs), "mem", 1, mem_count)
+    split = padded // LANES // 2 * LANES
+    far_rounds = range(2, chips)
     outs = pl.pallas_call(
-        lambda *refs: code_kernel(width, *refs),
+        lambda *refs: code_kernel(width, split, *refs),
         in_specs=[VMEM] * 2,
-        out_specs=[VMEM] * chips,
-        out_shape=[jax.ShapeDtypeStruct((block, padded), jnp.float32)]
-        + [jax.ShapeDtypeStruct((block, padded), jnp.int16)] * (chips - 1),
+        out_specs=[VMEM] * (2 + 2 * len(far_rounds)),
+        out_shape=[
+            jax.ShapeDtypeStruct((block, padded), jnp.float32),
+            jax.ShapeDtypeStruct((block, padded), jnp.int16),
+        ]
+        + [jax.ShapeDtypeStruct((block, split + LANES), jnp.int16) for r in far_rounds]
+        + [jax.ShapeDtypeStruct((block, padded - split), jnp.int16 if r % 2 else jnp.float32) for r in far_rounds],
         compiler_params=pltpu.CompilerParams(vmem_limit_bytes=16 * 2**20),
     )(multiply(kept_lhs), theirs)
-
-    arrived = [swap(outs[r], "mem", 2 * r, mem_count) for r in range(1, chips)]
+    own, beside_code = outs[:2]
+    lows = dict(zip(far_rounds, outs[2:]))
+    highs = dict(zip(far_rounds, outs[2 + len(far_rounds):]))
+    evens = [r for r in far_rounds if r % 2 == 0]
+
+    helped = [swap(highs[r + 1], "mem", 2, mem_count) for r in evens]
+    arrived = [swap(lows[r], "mem", 2 * r, mem_count) for r in far_rounds]
+    near_arrived = swap(beside_code, "mem", 2, mem_count)
+    relayed = pl.pallas_call(
+        lambda *refs: relay_kernel(width, split, *refs),
+        in_specs=[VMEM] * (2 * len(evens)),
+        out_specs=[VMEM] * len(evens),
+        out_shape=[jax.ShapeDtypeStruct((block, padded - split), jnp.int16)] * len(evens),
+        compiler_params=pltpu.CompilerParams(vmem_limit_bytes=8 * 2**20),
+    )(*[highs[r] for r in evens], *helped)
+    high_arrived = [swap(relayed[i], "mem", 2 * r, mem_count) for i, r in enumerate(evens)]
     return pl.pallas_call(
-        lambda *refs: combine_kernel(width, *refs),
+        lambda *refs: combine_kernel(width, split, *refs),
+        in_specs=[VMEM] * (2 + len(far_rounds) + len(evens)),
+        out_specs=VMEM,
         out_shape=jax.ShapeDtypeStruct((block, width), jnp.float32),
         compiler_params=pltpu.CompilerParams(vmem_limit_bytes=8 * 2**20),
-    )(outs[0], *arrived)
+    )(own, near_arrived, *arrived, *high_arrived)
 
 
 def solution(mesh):

time: 63.7 us -> 60.2 us (0.945)
  the two profiles are of different devices: /device:TPU:8 before, /device:TPU:0 now
where the time goes in v3:
time: 60.2 us; the launch traced here: 60 us
  starting transfers between devices  19.4 us (32%)
  waiting for transfers between devices  18.8 us (31%)
  Pallas kernels  15.7 us (26%)
  other arithmetic  3.03 us (5%)
  local copies, waits for them, and re-layouts  2.77 us (5%)
    ppermute x16, starting transfers between devices, swap(): return lax.ppermute(x, axis, [(i, i ^ k) for i in range(count)])  19.4 us
    ppermute x16, waiting for transfers between devices, swap(): return lax.ppermute(x, axis, [(i, i ^ k) for i in range(count)])  18.8 us
    pallas_call x2, Pallas kernels, mask(): pl.pallas_call(lambda *refs: mask_kernel(base, *refs), in_specs=[SMEM, SM...  7.13 us
    pallas_call x2, Pallas kernels, multiply(): pl.pallas_call(lambda *refs: dot_kernel(grp_count, *refs), in_specs=[SMEM...  6.04 us
  transfers between devices with their start and end apart: 16, of which 8 were waited for; matrix products, arithmetic and copies ran while one was open for 3% of the time, Pallas kernels for 18%

profile of v3, /device:TPU:0, one launch (start us, length us, event | category | flops | bytes accessed | tf_op | source)
XLA Modules:
  0.0 60.0 jit_solution(3287417948392639381)
XLA Ops:
  0.0 1.1 %reshape.73 = bf16[10,4,2,4,600]{4,3,2,1,0:T(4,128)(2,1)S(1)} reshape(bf16[10,32,600]{2,1,0:T(8,128)(2,1)} %param.3) | data formatting | bytes 768000 | tf_op jit(solution)/shard_map/reshape | solution.py:196
  1.7 1.1 %collective-permute-done = bf16[10,4,4,600]{3,2,1,0:T(4,128)(2,1)S(1)} collective-permute-done((bf16[10,4,4,600]{3,2,1,0:T(4,128)(2,1)S(1)}, bf16[10,4,4,600]{3,2,1,0:T(4,128)(2,1)S(1)}, u32[]{:S(2)}, u32[]{:S(2)}) %collective-permute-start) | collective-permute-done | bytes 192032 | tf_op jit(solution)/shard_map/ppermute | solution.py:173
  3.3 3.0 %collective-permute-start.6 = (bf16[20,4,600]{2,1,0:T(4,128)(2,1)S(1)}, bf16[20,4,600]{2,1,0:T(4,128)(2,1)S(1)}, u32[]{:S(2)}, u32[]{:S(2)}) collective-permute-start(bf16[20,4,600]{2,1,0:T(4,128)(2,1)S(1)} %get-tuple-element.60), channel_id=1, source_target_pairs={{0,2},{1,3},{2,0},{3,1},{4,6},{5,7},{6,4},{7,5},{8,10},{9,11},{10,... | collective-permute-start | bytes 288008 | tf_op jit(solution)/shard_map/ppermute | solution.py:173
  6.3 0.7 %reshape.74.refs_2_ = s32[1,600]{1,0:T(1,128)S(1)} reshape(s32[600]{0:T(1024)} %refs_1_.3) | data formatting | bytes 4800 | tf_op jit(solution)/shard_map/reshape | solution.py:193
  7.0 2.6 %collective-permute-start.1 = (bf16[20,4,600]{2,1,0:T(4,128)(2,1)S(1)}, bf16[20,4,600]{2,1,0:T(4,128)(2,1)S(1)}, u32[]{:S(2)}, u32[]{:S(2)}) collective-permute-start(bf16[20,4,600]{2,1,0:T(4,128)(2,1)S(1)} %get-tuple-element.58), channel_id=1, source_target_pairs={{0,4},{1,5},{2,6},{3,7},{4,0},{5,1},{6,2},{7,3},{8,12},{9,13},{10,... | collective-permute-start | bytes 288008 | tf_op jit(solution)/shard_map/ppermute | solution.py:173
  9.7 2.7 %collective-permute-start.9 = (bf16[40,4,600]{2,1,0:T(4,128)(2,1)S(1)}, bf16[40,4,600]{2,1,0:T(4,128)(2,1)S(1)}, u32[]{:S(2)}, u32[]{:S(2)}) collective-permute-start(bf16[40,4,600]{2,1,0:T(4,128)(2,1)S(1)} %pad_maximum_fusion.1), channel_id=1, source_target_pairs={{0,24},{8,16},{16,8},{24,0},{1,25},{9,17},{17,9},{25,1},{2,26},{10... | collective-permute-start | bytes 576008 | tf_op jit(solution)/shard_map/ppermute | solution.py:173
  13.4 4.4 %collective-permute-done.1 = bf16[20,4,600]{2,1,0:T(4,128)(2,1)S(1)} collective-permute-done((bf16[20,4,600]{2,1,0:T(4,128)(2,1)S(1)}, bf16[20,4,600]{2,1,0:T(4,128)(2,1)S(1)}, u32[]{:S(2)}, u32[]{:S(2)}) %collective-permute-start.1) | collective-permute-done | bytes 96032 | tf_op jit(solution)/shard_map/ppermute | solution.py:173
  17.9 2.5 %collective-permute-start.5 = (bf16[40,4,600]{2,1,0:T(4,128)(2,1)S(1)}, bf16[40,4,600]{2,1,0:T(4,128)(2,1)S(1)}, u32[]{:S(2)}, u32[]{:S(2)}) collective-permute-start(bf16[40,4,600]{2,1,0:T(4,128)(2,1)S(1)} %pad_maximum_fusion), channel_id=1, source_target_pairs={{0,24},{8,16},{16,8},{24,0},{1,25},{9,17},{17,9},{25,1},{2,26},{10... | collective-permute-start | bytes 576008 | tf_op jit(solution)/shard_map/ppermute | solution.py:173
  21.6 0.7 %copy-done = s32[600]{0:T(1024)S(1)} copy-done((s32[600]{0:T(1024)S(1)}, s32[600]{0:T(1024)}, u32[]{:S(2)}) %copy-start) | copy-done | bytes 2424
  22.3 3.6 %shard_map.37.refs_5_ = bf16[2,640,2432]{2,1,0:T(8,128)(2,1)S(1)} custom-call(s32[2]{0:T(128)S(1)} %pad_add_fusion.2.refs_0_, s32[600]{0:T(1024)S(1)} %copy-done, s32[1,600]{1,0:T(1,128)S(1)} %reshape.74.refs_2_, bf16[4,600,2400]{2,1,0:T(8,128)(2,1)} %bitcast.48), custom_call_target="tpu_custom_call" | custom-call | bytes 11520000 | tf_op jit(solution)/shard_map/pallas_call | solution.py:180
  25.9 3.6 %shard_map.38.refs_6_ = bf16[2,640,2432]{2,1,0:T(8,128)(2,1)S(1)} custom-call(s32[2]{0:T(128)S(1)} %pad_add_fusion.1.refs_0_, s32[600]{0:T(1024)S(1)} %copy-done.1, s32[1,600]{1,0:T(1,128)S(1)} %reshape.74.refs_2_, bf16[4,600,2400]{2,1,0:T(8,128)(2,1)} %bitcast.49), custom_call_target="tpu_custom_call" | custom-call | bytes 11520000 | tf_op jit(solution)/shard_map/pallas_call | solution.py:180
  29.5 0.9 %collective-permute-done.4 = bf16[40,4,600]{2,1,0:T(4,128)(2,1)S(1)} collective-permute-done((bf16[40,4,600]{2,1,0:T(4,128)(2,1)S(1)}, bf16[40,4,600]{2,1,0:T(4,128)(2,1)S(1)}, u32[]{:S(2)}, u32[]{:S(2)}) %collective-permute-start.4) | collective-permute-done | bytes 192032 | tf_op jit(solution)/shard_map/ppermute | solution.py:173
  32.4 3.0 %shard_map.40 = f32[160,2432]{1,0:T(8,128)S(1)} custom-call(s32[3]{0:T(128)S(1)} %pad_add_fusion.refs_0_, bf16[40,2560]{1,0:T(8,128)(2,1)S(1)} %bitcast.43, bf16[40,2560]{1,0:T(8,128)(2,1)S(1)} %bitcast.41, bf16[40,2560]{1,0:T(8,128)(2,1)S(1)} %bitcast.47, bf16[40,2560]{1,0:T(8,128)(2,1)S(1)} %bitcast.45, bf16[2,640,2432]{2,1,0:T(8,128)(2,1)S(1)} %shard_map.37.refs_5_, ...), custom_call_target="tpu_custom_call" | custom-call | flops 1843200000 | bytes 1536000 | tf_op jit(solution)/shard_map/pallas_call | solution.py:245
  36.1 3.0 %shard_map.39.refs_0_ = f32[160,2432]{1,0:T(8,128)S(1)} custom-call(s32[3]{0:T(128)S(1)} %pad_add_fusion.refs_0_, bf16[40,2560]{1,0:T(8,128)(2,1)S(1)} %bitcast.42, bf16[40,2560]{1,0:T(8,128)(2,1)S(1)} %bitcast.40, bf16[40,2560]{1,0:T(8,128)(2,1)S(1)} %bitcast.44, bf16[40,2560]{1,0:T(8,128)(2,1)S(1)} %bitcast.46, ...), custom_call_target="tpu_custom_call" | custom-call | flops 1843200000 | bytes 1536000 | tf_op jit(solution)/shard_map/pallas_call | solution.py:245
  39.1 0.7 %shard_map.41 = (f32[40,2432]{1,0:T(8,128)S(1)}, s16[40,2432]{1,0:T(8,128)(2,1)S(1)}, s16[40,1280]{1,0:T(8,128)(2,1)S(1)}, s16[40,1280]{1,0:T(8,128)(2,1)S(1)}, ...) custom-call(f32[160,2432]{1,0:T(8,128)S(1)} %shard_map.39.refs_0_, f32[160,2432]{1,0:T(8,128)S(1)} %collective-permute-done.10.refs_1_), custom_call_target="tpu_custom_call" | custom-call | tf_op jit(solution)/shard_map/pallas_call | solution.py:261
  39.8 1.4 %collective-permute-start.14 = (s16[40,1280]{1,0:T(8,128)(2,1)S(1)}, s16[40,1280]{1,0:T(8,128)(2,1)S(1)}, u32[]{:S(2)}, u32[]{:S(2)}) collective-permute-start(s16[40,1280]{1,0:T(8,128)(2,1)S(1)} %get-tuple-element.42), channel_id=1, source_target_pairs={{0,2},{1,3},{2,0},{3,1},{4,6},{5,7},{6,4},{7,5},{8,10},{9,11},{10,... | collective-permute-start | bytes 307208 | tf_op jit(solution)/shard_map/ppermute | solution.py:173
  41.9 2.4 %collective-permute-start.12 = (s16[40,1280]{1,0:T(8,128)(2,1)S(1)}, s16[40,1280]{1,0:T(8,128)(2,1)S(1)}, u32[]{:S(2)}, u32[]{:S(2)}) collective-permute-start(s16[40,1280]{1,0:T(8,128)(2,1)S(1)} %get-tuple-element.39), channel_id=1, source_target_pairs={{0,4},{1,5},{2,6},{3,7},{4,0},{5,1},{6,2},{7,3},{8,12},{9,13},{10,... | collective-permute-start | bytes 307208 | tf_op jit(solution)/shard_map/ppermute | solution.py:173
  44.3 1.4 %collective-permute-start.13 = (s16[40,1280]{1,0:T(8,128)(2,1)S(1)}, s16[40,1280]{1,0:T(8,128)(2,1)S(1)}, u32[]{:S(2)}, u32[]{:S(2)}) collective-permute-start(s16[40,1280]{1,0:T(8,128)(2,1)S(1)} %get-tuple-element.40), channel_id=1, source_target_pairs={{0,6},{1,7},{2,4},{3,5},{4,2},{5,3},{6,0},{7,1},{8,14},{9,15},{10,... | collective-permute-start | bytes 307208 | tf_op jit(solution)/shard_map/ppermute | solution.py:173
  45.7 2.1 %collective-permute-done.14.refs_1_ = s16[40,1280]{1,0:T(8,128)(2,1)S(1)} collective-permute-done((s16[40,1280]{1,0:T(8,128)(2,1)S(1)}, s16[40,1280]{1,0:T(8,128)(2,1)S(1)}, u32[]{:S(2)}, u32[]{:S(2)}) %collective-permute-start.14) | collective-permute-done | bytes 102432 | tf_op jit(solution)/shard_map/ppermute | solution.py:173
  47.8 0.7 %shard_map.42 = s16[40,1280]{1,0:T(8,128)(2,1)S(1)} custom-call(f32[40,1280]{1,0:T(8,128)S(1)} %get-tuple-element.41.refs_0_, s16[40,1280]{1,0:T(8,128)(2,1)S(1)} %collective-permute-done.14.refs_1_), custom_call_target="tpu_custom_call" | custom-call | tf_op jit(solution)/shard_map/pallas_call | solution.py:281
  48.8 2.1 %collective-permute-done.12.refs_2_ = s16[40,1280]{1,0:T(8,128)(2,1)S(1)} collective-permute-done((s16[40,1280]{1,0:T(8,128)(2,1)S(1)}, s16[40,1280]{1,0:T(8,128)(2,1)S(1)}, u32[]{:S(2)}, u32[]{:S(2)}) %collective-permute-start.12) | collective-permute-done | bytes 102432 | tf_op jit(solution)/shard_map/ppermute | solution.py:173
  50.9 5.2 %collective-permute-done.13.refs_3_ = s16[40,1280]{1,0:T(8,128)(2,1)S(1)} collective-permute-done((s16[40,1280]{1,0:T(8,128)(2,1)S(1)}, s16[40,1280]{1,0:T(8,128)(2,1)S(1)}, u32[]{:S(2)}, u32[]{:S(2)}) %collective-permute-start.13) | collective-permute-done | bytes 102432 | tf_op jit(solution)/shard_map/ppermute | solution.py:173
  56.1 2.8 %collective-permute-done.15.refs_4_ = s16[40,1280]{1,0:T(8,128)(2,1)S(1)} collective-permute-done((s16[40,1280]{1,0:T(8,128)(2,1)S(1)}, s16[40,1280]{1,0:T(8,128)(2,1)S(1)}, u32[]{:S(2)}, u32[]{:S(2)}) %collective-permute-start.15) | collective-permute-done | bytes 102432 | tf_op jit(solution)/shard_map/ppermute | solution.py:173
  58.9 1.1 %shard_map.43 = f32[40,2400]{1,0:T(8,128)} custom-call(f32[40,2432]{1,0:T(8,128)S(1)} %get-tuple-element.37.refs_0_, s16[40,2432]{1,0:T(8,128)(2,1)S(1)} %collective-permute-done.11.refs_1_, s16[40,1280]{1,0:T(8,128)(2,1)S(1)} %collective-permute-done.12.refs_2_, s16[40,1280]{1,0:T(8,128)(2,1)S(1)} %collective-permute-done.13.refs_3_, ...), custom_call_target="tpu_custom_call" | custom-call | tf_op jit(solution)/shard_map/pallas_call | solution.py:289
  (51 shorter events, 6.8 us)
Async XLA Ops:
  1.2 1.6 %collective-permute-start = (bf16[10,4,4,600]{3,2,1,0:T(4,128)(2,1)S(1)}, bf16[10,4,4,600]{3,2,1,0:T(4,128)(2,1)S(1)}, u32[]{:S(2)}, u32[]{:S(2)}) collective-permute-start(bf16[10,4,4,600]{3,2,1,0:T(4,128)(2,1)S(1)} %dynamic-slice_bitcast_fusion), channel_id=1, source_target_pairs={{0,1},{1,0},{2,3},{3,2},{4,5},{5,4},{6,7},{7,6},{8,9},{9,8},{10,11... | collective-permute-start | bytes 576008 | tf_op jit(solution)/shard_map/ppermute | solution.py:173
  3.3 6.3 %collective-permute-start.6 = (bf16[20,4,600]{2,1,0:T(4,128)(2,1)S(1)}, bf16[20,4,600]{2,1,0:T(4,128)(2,1)S(1)}, u32[]{:S(2)}, u32[]{:S(2)}) collective-permute-start(bf16[20,4,600]{2,1,0:T(4,128)(2,1)S(1)} %get-tuple-element.60), channel_id=1, source_target_pairs={{0,2},{1,3},{2,0},{3,1},{4,6},{5,7},{6,4},{7,5},{8,10},{9,11},{10,... | collective-permute-start | bytes 288008 | tf_op jit(solution)/shard_map/ppermute | solution.py:173
  7.0 10.8 %collective-permute-start.1 = (bf16[20,4,600]{2,1,0:T(4,128)(2,1)S(1)}, bf16[20,4,600]{2,1,0:T(4,128)(2,1)S(1)}, u32[]{:S(2)}, u32[]{:S(2)}) collective-permute-start(bf16[20,4,600]{2,1,0:T(4,128)(2,1)S(1)} %get-tuple-element.58), channel_id=1, source_target_pairs={{0,4},{1,5},{2,6},{3,7},{4,0},{5,1},{6,2},{7,3},{8,12},{9,13},{10,... | collective-permute-start | bytes 288008 | tf_op jit(solution)/shard_map/ppermute | solution.py:173
  9.6 8.2 %collective-permute-start.2 = (bf16[20,4,600]{2,1,0:T(4,128)(2,1)S(1)}, bf16[20,4,600]{2,1,0:T(4,128)(2,1)S(1)}, u32[]{:S(2)}, u32[]{:S(2)}) collective-permute-start(bf16[20,4,600]{2,1,0:T(4,128)(2,1)S(1)} %get-tuple-element.59), channel_id=1, source_target_pairs={{0,6},{1,7},{2,4},{3,5},{4,2},{5,3},{6,0},{7,1},{8,14},{9,15},{10,... | collective-permute-start | bytes 288008 | tf_op jit(solution)/shard_map/ppermute | solution.py:173
  9.7 11.2 %collective-permute-start.9 = (bf16[40,4,600]{2,1,0:T(4,128)(2,1)S(1)}, bf16[40,4,600]{2,1,0:T(4,128)(2,1)S(1)}, u32[]{:S(2)}, u32[]{:S(2)}) collective-permute-start(bf16[40,4,600]{2,1,0:T(4,128)(2,1)S(1)} %pad_maximum_fusion.1), channel_id=1, source_target_pairs={{0,24},{8,16},{16,8},{24,0},{1,25},{9,17},{17,9},{25,1},{2,26},{10... | collective-permute-start | bytes 576008 | tf_op jit(solution)/shard_map/ppermute | solution.py:173
  12.5 13.3 %collective-permute-start.8 = (bf16[40,4,600]{2,1,0:T(4,128)(2,1)S(1)}, bf16[40,4,600]{2,1,0:T(4,128)(2,1)S(1)}, u32[]{:S(2)}, u32[]{:S(2)}) collective-permute-start(bf16[40,4,600]{2,1,0:T(4,128)(2,1)S(1)} %pad_maximum_fusion.1), channel_id=1, source_target_pairs={{0,16},{8,24},{16,0},{24,8},{1,17},{9,25},{17,1},{25,9},{2,18},{10... | collective-permute-start | bytes 576008 | tf_op jit(solution)/shard_map/ppermute | solution.py:173
  13.0 12.8 %collective-permute-start.7 = (bf16[40,4,600]{2,1,0:T(4,128)(2,1)S(1)}, bf16[40,4,600]{2,1,0:T(4,128)(2,1)S(1)}, u32[]{:S(2)}, u32[]{:S(2)}) collective-permute-start(bf16[40,4,600]{2,1,0:T(4,128)(2,1)S(1)} %pad_maximum_fusion.1), channel_id=1, source_target_pairs={{0,8},{8,0},{16,24},{24,16},{1,9},{9,1},{17,25},{25,17},{2,10},{10... | collective-permute-start | bytes 576008 | tf_op jit(solution)/shard_map/ppermute | solution.py:173
  17.9 11.6 %collective-permute-start.5 = (bf16[40,4,600]{2,1,0:T(4,128)(2,1)S(1)}, bf16[40,4,600]{2,1,0:T(4,128)(2,1)S(1)}, u32[]{:S(2)}, u32[]{:S(2)}) collective-permute-start(bf16[40,4,600]{2,1,0:T(4,128)(2,1)S(1)} %pad_maximum_fusion), channel_id=1, source_target_pairs={{0,24},{8,16},{16,8},{24,0},{1,25},{9,17},{17,9},{25,1},{2,26},{10... | collective-permute-start | bytes 576008 | tf_op jit(solution)/shard_map/ppermute | solution.py:173
  20.4 10.0 %collective-permute-start.4 = (bf16[40,4,600]{2,1,0:T(4,128)(2,1)S(1)}, bf16[40,4,600]{2,1,0:T(4,128)(2,1)S(1)}, u32[]{:S(2)}, u32[]{:S(2)}) collective-permute-start(bf16[40,4,600]{2,1,0:T(4,128)(2,1)S(1)} %pad_maximum_fusion), channel_id=1, source_target_pairs={{0,16},{8,24},{16,0},{24,8},{1,17},{9,25},{17,1},{25,9},{2,18},{10... | collective-permute-start | bytes 576008 | tf_op jit(solution)/shard_map/ppermute | solution.py:173
  20.9 9.6 %collective-permute-start.3 = (bf16[40,4,600]{2,1,0:T(4,128)(2,1)S(1)}, bf16[40,4,600]{2,1,0:T(4,128)(2,1)S(1)}, u32[]{:S(2)}, u32[]{:S(2)}) collective-permute-start(bf16[40,4,600]{2,1,0:T(4,128)(2,1)S(1)} %pad_maximum_fusion), channel_id=1, source_target_pairs={{0,8},{8,0},{16,24},{24,16},{1,9},{9,1},{17,25},{25,17},{2,10},{10... | collective-permute-start | bytes 576008 | tf_op jit(solution)/shard_map/ppermute | solution.py:173
  21.6 0.7 %copy-start = (s32[600]{0:T(1024)S(1)}, s32[600]{0:T(1024)}, u32[]{:S(2)}) copy-start(s32[600]{0:T(1024)} %refs_1_.3) | copy-start | bytes 7204
  22.3 3.6 %copy-start.1 = (s32[600]{0:T(1024)S(1)}, s32[600]{0:T(1024)}, u32[]{:S(2)}) copy-start(s32[600]{0:T(1024)} %refs_1_.3) | copy-start | bytes 7204
  35.4 3.7 %collective-permute-start.10 = (f32[160,2432]{1,0:T(8,128)S(1)}, f32[160,2432]{1,0:T(8,128)S(1)}, u32[]{:S(2)}, u32[]{:S(2)}) collective-permute-start(f32[160,2432]{1,0:T(8,128)S(1)} %shard_map.40), channel_id=1, source_target_pairs={{0,1},{1,0},{2,3},{3,2},{4,5},{5,4},{6,7},{7,6},{8,9},{9,8},{10,11... | collective-permute-start | bytes 4669448 | tf_op jit(solution)/shard_map/ppermute | solution.py:173
  39.8 7.9 %collective-permute-start.14 = (s16[40,1280]{1,0:T(8,128)(2,1)S(1)}, s16[40,1280]{1,0:T(8,128)(2,1)S(1)}, u32[]{:S(2)}, u32[]{:S(2)}) collective-permute-start(s16[40,1280]{1,0:T(8,128)(2,1)S(1)} %get-tuple-element.42), channel_id=1, source_target_pairs={{0,2},{1,3},{2,0},{3,1},{4,6},{5,7},{6,4},{7,5},{8,10},{9,11},{10,... | collective-permute-start | bytes 307208 | tf_op jit(solution)/shard_map/ppermute | solution.py:173
  41.3 14.8 %collective-permute-start.11 = (s16[40,2432]{1,0:T(8,128)(2,1)S(1)}, s16[40,2432]{1,0:T(8,128)(2,1)S(1)}, u32[]{:S(2)}, u32[]{:S(2)}) collective-permute-start(s16[40,2432]{1,0:T(8,128)(2,1)S(1)} %get-tuple-element.38), channel_id=1, source_target_pairs={{0,2},{1,3},{2,0},{3,1},{4,6},{5,7},{6,4},{7,5},{8,10},{9,11},{10,... | collective-permute-start | bytes 583688 | tf_op jit(solution)/shard_map/ppermute | solution.py:173
  41.9 8.9 %collective-permute-start.12 = (s16[40,1280]{1,0:T(8,128)(2,1)S(1)}, s16[40,1280]{1,0:T(8,128)(2,1)S(1)}, u32[]{:S(2)}, u32[]{:S(2)}) collective-permute-start(s16[40,1280]{1,0:T(8,128)(2,1)S(1)} %get-tuple-element.39), channel_id=1, source_target_pairs={{0,4},{1,5},{2,6},{3,7},{4,0},{5,1},{6,2},{7,3},{8,12},{9,13},{10,... | collective-permute-start | bytes 307208 | tf_op jit(solution)/shard_map/ppermute | solution.py:173
  44.3 11.7 %collective-permute-start.13 = (s16[40,1280]{1,0:T(8,128)(2,1)S(1)}, s16[40,1280]{1,0:T(8,128)(2,1)S(1)}, u32[]{:S(2)}, u32[]{:S(2)}) collective-permute-start(s16[40,1280]{1,0:T(8,128)(2,1)S(1)} %get-tuple-element.40), channel_id=1, source_target_pairs={{0,6},{1,7},{2,4},{3,5},{4,2},{5,3},{6,0},{7,1},{8,14},{9,15},{10,... | collective-permute-start | bytes 307208 | tf_op jit(solution)/shard_map/ppermute | solution.py:173
  48.5 10.4 %collective-permute-start.15 = (s16[40,1280]{1,0:T(8,128)(2,1)S(1)}, s16[40,1280]{1,0:T(8,128)(2,1)S(1)}, u32[]{:S(2)}, u32[]{:S(2)}) collective-permute-start(s16[40,1280]{1,0:T(8,128)(2,1)S(1)} %shard_map.42), channel_id=1, source_target_pairs={{0,4},{1,5},{2,6},{3,7},{4,0},{5,1},{6,2},{7,3},{8,12},{9,13},{10,... | collective-permute-start | bytes 307208 | tf_op jit(solution)/shard_map/ppermute | solution.py:173

commit v4 on v3

--- a/solution.py
+++ b/solution.py
@@ -53,18 +53,18 @@
 
 
 def dot_kernel(grp_count, where_ref, *refs):
-    lhs_refs, part_refs = refs[:grp_count], refs[grp_count:-3]
-    out_ref, wide, lhs = refs[-3:]
+    lhs_refs, part_refs = refs[:grp_count], refs[grp_count:-2]
+    out_ref, lhs = refs[-2:]
     group, chip = where_ref[0], where_ref[1]
     rows_each = lhs_refs[0].shape[0]
     per_group = where_ref.shape[0] - 2
     block = rows_each // per_group
+    places = []
     for j in range(grp_count):
+        lhs[j * rows_each:(j + 1) * rows_each, :] = lhs_refs[j][...]
         for q in range(per_group):
             at = jnp.bitwise_xor(jnp.bitwise_xor(group, j) * per_group + q, chip)
-            rows = lhs_refs[j][q * block:(q + 1) * block, :].astype(jnp.float32)
-            wide[pl.ds(pl.multiple_of(at * block, 8), block), :] = rows
-    lhs[...] = wide[...].astype(jnp.bfloat16)
+            places.append(pl.ds(pl.multiple_of(at * block, 8), block))
     padded = out_ref.shape[1]
     size = part_refs[0].shape[0] * part_refs[0].shape[1]
     for first in range(0, padded, TILE_N):
@@ -74,7 +74,8 @@
             right = part_ref[:, :, first:last].reshape(size, last - first)
             term = jnp.dot(lhs[:, i * size:(i + 1) * size], right, preferred_element_type=jnp.float32)
             total = term if total is None else total + term
-        out_ref[:, first:last] = total
+        for i, rows in enumerate(places):
+            out_ref[rows, first:last] = total[i * block:(i + 1) * block]
 
 
 def encode(part, lane, at, exponents):
@@ -211,10 +212,18 @@
     def around(x):
         return [x] + [swap(x, "grp", k, grp_count) for k in range(1, grp_count)]
 
-    x = jnp.concatenate(got[:chips // 2])
-    y = jnp.concatenate(got[chips // 2:])
+    def in_order(some):
+        bit = 1
+        while bit < len(some):
+            flip = jnp.bitwise_and(chip, bit) != 0
+            some = [jnp.where(flip, some[j ^ bit], some[j]) for j in range(len(some))]
+            bit *= 2
+        return jnp.concatenate(some)
+
+    x = in_order(got[:chips // 2])
+    y = in_order(got[chips // 2:])
     x_all = around(x)
-    y, late = lax.optimization_barrier((y, vvvv))
+    y, late, x_all[3] = lax.optimization_barrier((y, vvvv, x_all[3]))
     parts = [mask(late, mem, 0, half // 2)]
     x_all, parts, late = lax.optimization_barrier((x_all, parts, late))
     y_all, part = lax.optimization_barrier((around(y), mask(late, mem, half // 2, half // 2)))
@@ -223,17 +232,18 @@
 
     pair_rows = 2 * per_device
     kept_lhs, lent_lhs = [], []
+    is_upper = chip // (chips // 2)
     for one, two in zip(*halves):
-        stack = jnp.concatenate([one, two]).reshape(chips, pair_rows, half, nv)
-        stack = [stack[j] for j in range(chips)]
-        bit = 1
-        while bit < chips:
-            flip = jnp.bitwise_and(chip, bit) != 0
-            stack = [jnp.where(flip, stack[j ^ bit], stack[j]) for j in range(chips)]
-            bit *= 2
         for lhs, target in ((kept_lhs, core), (lent_lhs, 1 - core)):
-            first = target == 0
-            rows = [jnp.where(first, stack[j], stack[j + hop]) for j in range(chips) if j // hop % 2 == 0]
+            if chips // 2 == hop:
+                rows = [jnp.where(is_upper == target, one, two)]
+            else:
+                near, far = [x.reshape(chips // 2, pair_rows, half, nv) for x in (one, two)]
+                wanted = target == 0
+                rows = []
+                for upper in (0, 1):
+                    stack = jnp.where(is_upper == upper, near, far)
+                    rows += [jnp.where(wanted, stack[j], stack[j + hop]) for j in range(chips // 2) if j // hop % 2 == 0]
             filled = jnp.pad(jnp.concatenate(rows), ((0, 0), (0, 0), (0, depth - nv)))
             lhs.append(filled.reshape(chips // 2 * pair_rows, half * depth))
 
@@ -247,10 +257,7 @@
             in_specs=[SMEM] + [VMEM] * (grp_count + len(parts)),
             out_specs=VMEM,
             out_shape=jax.ShapeDtypeStruct((rows, padded), jnp.float32),
-            scratch_shapes=[
-                pltpu.VMEM((rows, half * depth), jnp.float32),
-                pltpu.VMEM((rows, half * depth), jnp.bfloat16),
-            ],
+            scratch_shapes=[pltpu.VMEM((rows, half * depth), jnp.bfloat16)],
             compiler_params=pltpu.CompilerParams(vmem_limit_bytes=round_up(rows * half * depth * 6, 2**20) + 6 * 2**20),
             cost_estimate=pl.CostEstimate(flops=2 * rows * half * nv * width, bytes_accessed=4 * rows * width, transcendentals=0),
         )(where, *lhs, *parts)
@@ -276,8 +283,8 @@
     evens = [r for r in far_rounds if r % 2 == 0]
 
     helped = [swap(highs[r + 1], "mem", 2, mem_count) for r in evens]
+    near_arrived = swap(beside_code, "mem", 2, mem_count)
     arrived = [swap(lows[r], "mem", 2 * r, mem_count) for r in far_rounds]
-    near_arrived = swap(beside_code, "mem", 2, mem_count)
     relayed = pl.pallas_call(
         lambda *refs: relay_kernel(width, split, *refs),
         in_specs=[VMEM] * (2 * len(evens)),

time: 60.2 us -> 58.9 us (0.978)
  starting transfers between devices: 19.4 us -> 22.2 us
  waiting for transfers between devices: 18.8 us -> 16.1 us
  other arithmetic: 3.03 us -> 1.29 us
  local copies, waits for them, and re-layouts: 2.77 us -> 3.49 us
    ppermute x16, starting transfers between devices: 19.4 us -> 22.2 us  [swap(): return lax.ppermute(x, axis, [(i, i ^ k) for i in range(count)])]
    ppermute x16, waiting for transfers between devices: 18.8 us -> 16.1 us  [swap(): return lax.ppermute(x, axis, [(i, i ^ k) for i in range(count)])]
    concatenate x10 -> x2, other arithmetic: 1.15 us -> 0.29 us  [in_order(): return jnp.concatenate(some)]
    select_n x6 -> x5, other arithmetic: 1.19 us -> 0.38 us  [the longest x3 0.2 us: in_order(): some = [jnp.where(flip, some[j ^ bit], some[j]) for j in range(len(some))]]
    pad x0 -> x8, local copies, waits for them, and re-layouts: none -> 0.72 us  [shards(): filled = jnp.pad(jnp.concatenate(rows), ((0, 0), (0, 0), (0, depth - nv)))]
  transfers between devices with their start and end apart: 16 -> 16, of which waited for: 8 -> 10; matrix products, arithmetic and copies ran while one was open for 3% -> 3% of each run, Pallas kernels for 18% -> 18%
where the time goes in v4:
time: 58.9 us; the launch traced here: 58.7 us
  starting transfers between devices  22.2 us (38%)
  waiting for transfers between devices  16.1 us (27%)
  Pallas kernels  15.3 us (26%)
  local copies, waits for them, and re-layouts  3.49 us (6%)
  other arithmetic  1.29 us (2%)
    ppermute x16, starting transfers between devices, swap(): return lax.ppermute(x, axis, [(i, i ^ k) for i in range(count)])  22.2 us
    ppermute x16, waiting for transfers between devices, swap(): return lax.ppermute(x, axis, [(i, i ^ k) for i in range(count)])  16.1 us
    pallas_call x2, Pallas kernels, mask(): pl.pallas_call(lambda *refs: mask_kernel(base, *refs), in_specs=[SMEM, SM...  7.13 us
    pallas_call x2, Pallas kernels, multiply(): pl.pallas_call(lambda *refs: dot_kernel(grp_count, *refs), in_specs=[SMEM...  5.66 us
  transfers between devices with their start and end apart: 16, of which 10 were waited for; matrix products, arithmetic and copies ran while one was open for 3% of the time, Pallas kernels for 18%

profile of v4, /device:TPU:0, one launch (start us, length us, event | category | flops | bytes accessed | tf_op | source)
XLA Modules:
  0.0 58.7 jit_solution(5795293381947140571)
XLA Ops:
  0.0 1.1 %reshape.37 = bf16[10,4,2,4,600]{4,3,2,1,0:T(4,128)(2,1)S(1)} reshape(bf16[10,32,600]{2,1,0:T(8,128)(2,1)} %param.3) | data formatting | bytes 768000 | tf_op jit(solution)/shard_map/reshape | solution.py:197
  1.7 0.7 %reshape.38.refs_2_ = s32[1,600]{1,0:T(1,128)S(1)} reshape(s32[600]{0:T(1024)} %refs_1_.3) | data formatting | bytes 4800 | tf_op jit(solution)/shard_map/reshape | solution.py:194
  3.2 3.0 %collective-permute-start.1 = (bf16[20,4,600]{2,1,0:T(4,128)(2,1)S(1)}, bf16[20,4,600]{2,1,0:T(4,128)(2,1)S(1)}, u32[]{:S(2)}, u32[]{:S(2)}) collective-permute-start(bf16[20,4,600]{2,1,0:T(4,128)(2,1)S(1)} %get-tuple-element.58), channel_id=1, source_target_pairs={{0,2},{1,3},{2,0},{3,1},{4,6},{5,7},{6,4},{7,5},{8,10},{9,11},{10,... | collective-permute-start | bytes 288008 | tf_op jit(solution)/shard_map/ppermute | solution.py:174
  6.3 2.5 %collective-permute-start.4 = (bf16[20,4,600]{2,1,0:T(4,128)(2,1)S(1)}, bf16[20,4,600]{2,1,0:T(4,128)(2,1)S(1)}, u32[]{:S(2)}, u32[]{:S(2)}) collective-permute-start(bf16[20,4,600]{2,1,0:T(4,128)(2,1)S(1)} %get-tuple-element.57), channel_id=1, source_target_pairs={{0,6},{1,7},{2,4},{3,5},{4,2},{5,3},{6,0},{7,1},{8,14},{9,15},{10,... | collective-permute-start | bytes 288008 | tf_op jit(solution)/shard_map/ppermute | solution.py:174
  9.7 2.7 %collective-permute-start.6 = (bf16[40,4,600]{2,1,0:T(4,128)(2,1)S(1)}, bf16[40,4,600]{2,1,0:T(4,128)(2,1)S(1)}, u32[]{:S(2)}, u32[]{:S(2)}) collective-permute-start(bf16[40,4,600]{2,1,0:T(4,128)(2,1)S(1)} %pad_maximum_fusion), channel_id=1, source_target_pairs={{0,24},{8,16},{16,8},{24,0},{1,25},{9,17},{17,9},{25,1},{2,26},{10... | collective-permute-start | bytes 576008 | tf_op jit(solution)/shard_map/ppermute | solution.py:174
  13.3 1.4 %collective-permute-done.4 = bf16[20,4,600]{2,1,0:T(4,128)(2,1)S(1)} collective-permute-done((bf16[20,4,600]{2,1,0:T(4,128)(2,1)S(1)}, bf16[20,4,600]{2,1,0:T(4,128)(2,1)S(1)}, u32[]{:S(2)}, u32[]{:S(2)}) %collective-permute-start.4) | collective-permute-done | bytes 96032 | tf_op jit(solution)/shard_map/ppermute | solution.py:174
  14.7 3.7 %collective-permute-done.5 = bf16[20,4,600]{2,1,0:T(4,128)(2,1)S(1)} collective-permute-done((bf16[20,4,600]{2,1,0:T(4,128)(2,1)S(1)}, bf16[20,4,600]{2,1,0:T(4,128)(2,1)S(1)}, u32[]{:S(2)}, u32[]{:S(2)}) %collective-permute-start.5) | collective-permute-done | bytes 96032 | tf_op jit(solution)/shard_map/ppermute | solution.py:174
  18.7 2.6 %collective-permute-start.9 = (bf16[40,4,600]{2,1,0:T(4,128)(2,1)S(1)}, bf16[40,4,600]{2,1,0:T(4,128)(2,1)S(1)}, u32[]{:S(2)}, u32[]{:S(2)}) collective-permute-start(bf16[40,4,600]{2,1,0:T(4,128)(2,1)S(1)} %pad_maximum_fusion.1), channel_id=1, source_target_pairs={{0,24},{8,16},{16,8},{24,0},{1,25},{9,17},{17,9},{25,1},{2,26},{10... | collective-permute-start | bytes 576008 | tf_op jit(solution)/shard_map/ppermute | solution.py:174
  22.4 0.7 %copy-done = s32[600]{0:T(1024)S(1)} copy-done((s32[600]{0:T(1024)S(1)}, s32[600]{0:T(1024)}, u32[]{:S(2)}) %copy-start) | copy-done | bytes 2424
  23.1 3.6 %shard_map.37.refs_5_ = bf16[2,640,2432]{2,1,0:T(8,128)(2,1)S(1)} custom-call(s32[2]{0:T(128)S(1)} %pad_add_fusion.1.refs_0_, s32[600]{0:T(1024)S(1)} %copy-done, s32[1,600]{1,0:T(1,128)S(1)} %reshape.38.refs_2_, bf16[4,600,2400]{2,1,0:T(8,128)(2,1)} %bitcast.69), custom_call_target="tpu_custom_call" | custom-call | bytes 11520000 | tf_op jit(solution)/shard_map/pallas_call | solution.py:181
  26.7 3.6 %shard_map.38.refs_6_ = bf16[2,640,2432]{2,1,0:T(8,128)(2,1)S(1)} custom-call(s32[2]{0:T(128)S(1)} %pad_add_fusion.2.refs_0_, s32[600]{0:T(1024)S(1)} %copy-done.1, s32[1,600]{1,0:T(1,128)S(1)} %reshape.38.refs_2_, bf16[4,600,2400]{2,1,0:T(8,128)(2,1)} %bitcast.70), custom_call_target="tpu_custom_call" | custom-call | bytes 11520000 | tf_op jit(solution)/shard_map/pallas_call | solution.py:181
  31.4 2.8 %shard_map.40 = f32[160,2432]{1,0:T(8,128)S(1)} custom-call(s32[3]{0:T(128)S(1)} %pad_add_fusion.refs_0_, bf16[40,2560]{1,0:T(8,128)(2,1)S(1)} %bitcast.65, bf16[40,2560]{1,0:T(8,128)(2,1)S(1)} %bitcast.66, bf16[40,2560]{1,0:T(8,128)(2,1)S(1)} %bitcast.61, bf16[40,2560]{1,0:T(8,128)(2,1)S(1)} %bitcast.68, bf16[2,640,2432]{2,1,0:T(8,128)(2,1)S(1)} %shard_map.37.refs_5_, ...), custom_call_target="tpu_custom_call" | custom-call | flops 1843200000 | bytes 1536000 | tf_op jit(solution)/shard_map/pallas_call | solution.py:255
  34.8 2.8 %shard_map.39.refs_0_ = f32[160,2432]{1,0:T(8,128)S(1)} custom-call(s32[3]{0:T(128)S(1)} %pad_add_fusion.refs_0_, bf16[40,2560]{1,0:T(8,128)(2,1)S(1)} %bitcast.63, bf16[40,2560]{1,0:T(8,128)(2,1)S(1)} %bitcast.64, bf16[40,2560]{1,0:T(8,128)(2,1)S(1)} %bitcast.62, bf16[40,2560]{1,0:T(8,128)(2,1)S(1)} %bitcast.67, ...), custom_call_target="tpu_custom_call" | custom-call | flops 1843200000 | bytes 1536000 | tf_op jit(solution)/shard_map/pallas_call | solution.py:255
  37.7 0.7 %shard_map.41 = (f32[40,2432]{1,0:T(8,128)S(1)}, s16[40,2432]{1,0:T(8,128)(2,1)S(1)}, s16[40,1280]{1,0:T(8,128)(2,1)S(1)}, s16[40,1280]{1,0:T(8,128)(2,1)S(1)}, ...) custom-call(f32[160,2432]{1,0:T(8,128)S(1)} %shard_map.39.refs_0_, f32[160,2432]{1,0:T(8,128)S(1)} %collective-permute-done.10.refs_1_), custom_call_target="tpu_custom_call" | custom-call | tf_op jit(solution)/shard_map/pallas_call | solution.py:268
  38.4 1.4 %collective-permute-start.14 = (s16[40,1280]{1,0:T(8,128)(2,1)S(1)}, s16[40,1280]{1,0:T(8,128)(2,1)S(1)}, u32[]{:S(2)}, u32[]{:S(2)}) collective-permute-start(s16[40,1280]{1,0:T(8,128)(2,1)S(1)} %get-tuple-element.44), channel_id=1, source_target_pairs={{0,2},{1,3},{2,0},{3,1},{4,6},{5,7},{6,4},{7,5},{8,10},{9,11},{10,... | collective-permute-start | bytes 307208 | tf_op jit(solution)/shard_map/ppermute | solution.py:174
  39.8 0.7 %collective-permute-start.11 = (s16[40,2432]{1,0:T(8,128)(2,1)S(1)}, s16[40,2432]{1,0:T(8,128)(2,1)S(1)}, u32[]{:S(2)}, u32[]{:S(2)}) collective-permute-start(s16[40,2432]{1,0:T(8,128)(2,1)S(1)} %get-tuple-element.40), channel_id=1, source_target_pairs={{0,2},{1,3},{2,0},{3,1},{4,6},{5,7},{6,4},{7,5},{8,10},{9,11},{10,... | collective-permute-start | bytes 583688 | tf_op jit(solution)/shard_map/ppermute | solution.py:174
  40.5 3.1 %collective-permute-start.12 = (s16[40,1280]{1,0:T(8,128)(2,1)S(1)}, s16[40,1280]{1,0:T(8,128)(2,1)S(1)}, u32[]{:S(2)}, u32[]{:S(2)}) collective-permute-start(s16[40,1280]{1,0:T(8,128)(2,1)S(1)} %get-tuple-element.41), channel_id=1, source_target_pairs={{0,4},{1,5},{2,6},{3,7},{4,0},{5,1},{6,2},{7,3},{8,12},{9,13},{10,... | collective-permute-start | bytes 307208 | tf_op jit(solution)/shard_map/ppermute | solution.py:174
  43.6 0.6 %collective-permute-start.13 = (s16[40,1280]{1,0:T(8,128)(2,1)S(1)}, s16[40,1280]{1,0:T(8,128)(2,1)S(1)}, u32[]{:S(2)}, u32[]{:S(2)}) collective-permute-start(s16[40,1280]{1,0:T(8,128)(2,1)S(1)} %get-tuple-element.42), channel_id=1, source_target_pairs={{0,6},{1,7},{2,4},{3,5},{4,2},{5,3},{6,0},{7,1},{8,14},{9,15},{10,... | collective-permute-start | bytes 307208 | tf_op jit(solution)/shard_map/ppermute | solution.py:174
  44.2 0.7 %shard_map.42 = s16[40,1280]{1,0:T(8,128)(2,1)S(1)} custom-call(f32[40,1280]{1,0:T(8,128)S(1)} %get-tuple-element.43.refs_0_, s16[40,1280]{1,0:T(8,128)(2,1)S(1)} %collective-permute-done.14.refs_1_), custom_call_target="tpu_custom_call" | custom-call | tf_op jit(solution)/shard_map/pallas_call | solution.py:288
  44.9 3.1 %collective-permute-start.15 = (s16[40,1280]{1,0:T(8,128)(2,1)S(1)}, s16[40,1280]{1,0:T(8,128)(2,1)S(1)}, u32[]{:S(2)}, u32[]{:S(2)}) collective-permute-start(s16[40,1280]{1,0:T(8,128)(2,1)S(1)} %shard_map.42), channel_id=1, source_target_pairs={{0,4},{1,5},{2,6},{3,7},{4,0},{5,1},{6,2},{7,3},{8,12},{9,13},{10,... | collective-permute-start | bytes 307208 | tf_op jit(solution)/shard_map/ppermute | solution.py:174
  48.0 1.4 %collective-permute-done.12.refs_2_ = s16[40,1280]{1,0:T(8,128)(2,1)S(1)} collective-permute-done((s16[40,1280]{1,0:T(8,128)(2,1)S(1)}, s16[40,1280]{1,0:T(8,128)(2,1)S(1)}, u32[]{:S(2)}, u32[]{:S(2)}) %collective-permute-start.12) | collective-permute-done | bytes 102432 | tf_op jit(solution)/shard_map/ppermute | solution.py:174
  49.4 5.9 %collective-permute-done.13.refs_3_ = s16[40,1280]{1,0:T(8,128)(2,1)S(1)} collective-permute-done((s16[40,1280]{1,0:T(8,128)(2,1)S(1)}, s16[40,1280]{1,0:T(8,128)(2,1)S(1)}, u32[]{:S(2)}, u32[]{:S(2)}) %collective-permute-start.13) | collective-permute-done | bytes 102432 | tf_op jit(solution)/shard_map/ppermute | solution.py:174
  55.3 2.2 %collective-permute-done.15.refs_4_ = s16[40,1280]{1,0:T(8,128)(2,1)S(1)} collective-permute-done((s16[40,1280]{1,0:T(8,128)(2,1)S(1)}, s16[40,1280]{1,0:T(8,128)(2,1)S(1)}, u32[]{:S(2)}, u32[]{:S(2)}) %collective-permute-start.15) | collective-permute-done | bytes 102432 | tf_op jit(solution)/shard_map/ppermute | solution.py:174
  57.6 1.1 %shard_map.43 = f32[40,2400]{1,0:T(8,128)} custom-call(f32[40,2432]{1,0:T(8,128)S(1)} %get-tuple-element.39.refs_0_, s16[40,2432]{1,0:T(8,128)(2,1)S(1)} %collective-permute-done.11.refs_1_, s16[40,1280]{1,0:T(8,128)(2,1)S(1)} %collective-permute-done.12.refs_2_, s16[40,1280]{1,0:T(8,128)(2,1)S(1)} %collective-permute-done.13.refs_3_, ...), custom_call_target="tpu_custom_call" | custom-call | tf_op jit(solution)/shard_map/pallas_call | solution.py:296
  (50 shorter events, 6.3 us)
Async XLA Ops:
  1.2 1.6 %collective-permute-start = (bf16[10,4,4,600]{3,2,1,0:T(4,128)(2,1)S(1)}, bf16[10,4,4,600]{3,2,1,0:T(4,128)(2,1)S(1)}, u32[]{:S(2)}, u32[]{:S(2)}) collective-permute-start(bf16[10,4,4,600]{3,2,1,0:T(4,128)(2,1)S(1)} %dynamic-slice_bitcast_fusion), channel_id=1, source_target_pairs={{0,1},{1,0},{2,3},{3,2},{4,5},{5,4},{6,7},{7,6},{8,9},{9,8},{10,11... | collective-permute-start | bytes 576008 | tf_op jit(solution)/shard_map/ppermute | solution.py:174
  3.2 6.2 %collective-permute-start.1 = (bf16[20,4,600]{2,1,0:T(4,128)(2,1)S(1)}, bf16[20,4,600]{2,1,0:T(4,128)(2,1)S(1)}, u32[]{:S(2)}, u32[]{:S(2)}) collective-permute-start(bf16[20,4,600]{2,1,0:T(4,128)(2,1)S(1)} %get-tuple-element.58), channel_id=1, source_target_pairs={{0,2},{1,3},{2,0},{3,1},{4,6},{5,7},{6,4},{7,5},{8,10},{9,11},{10,... | collective-permute-start | bytes 288008 | tf_op jit(solution)/shard_map/ppermute | solution.py:174
  6.3 8.4 %collective-permute-start.4 = (bf16[20,4,600]{2,1,0:T(4,128)(2,1)S(1)}, bf16[20,4,600]{2,1,0:T(4,128)(2,1)S(1)}, u32[]{:S(2)}, u32[]{:S(2)}) collective-permute-start(bf16[20,4,600]{2,1,0:T(4,128)(2,1)S(1)} %get-tuple-element.57), channel_id=1, source_target_pairs={{0,6},{1,7},{2,4},{3,5},{4,2},{5,3},{6,0},{7,1},{8,14},{9,15},{10,... | collective-permute-start | bytes 288008 | tf_op jit(solution)/shard_map/ppermute | solution.py:174
  8.8 9.6 %collective-permute-start.5 = (bf16[20,4,600]{2,1,0:T(4,128)(2,1)S(1)}, bf16[20,4,600]{2,1,0:T(4,128)(2,1)S(1)}, u32[]{:S(2)}, u32[]{:S(2)}) collective-permute-start(bf16[20,4,600]{2,1,0:T(4,128)(2,1)S(1)} %get-tuple-element.59), channel_id=1, source_target_pairs={{0,4},{1,5},{2,6},{3,7},{4,0},{5,1},{6,2},{7,3},{8,12},{9,13},{10,... | collective-permute-start | bytes 288008 | tf_op jit(solution)/shard_map/ppermute | solution.py:174
  9.7 9.0 %collective-permute-start.6 = (bf16[40,4,600]{2,1,0:T(4,128)(2,1)S(1)}, bf16[40,4,600]{2,1,0:T(4,128)(2,1)S(1)}, u32[]{:S(2)}, u32[]{:S(2)}) collective-permute-start(bf16[40,4,600]{2,1,0:T(4,128)(2,1)S(1)} %pad_maximum_fusion), channel_id=1, source_target_pairs={{0,24},{8,16},{16,8},{24,0},{1,25},{9,17},{17,9},{25,1},{2,26},{10... | collective-permute-start | bytes 576008 | tf_op jit(solution)/shard_map/ppermute | solution.py:174
  12.4 14.2 %collective-permute-start.3 = (bf16[40,4,600]{2,1,0:T(4,128)(2,1)S(1)}, bf16[40,4,600]{2,1,0:T(4,128)(2,1)S(1)}, u32[]{:S(2)}, u32[]{:S(2)}) collective-permute-start(bf16[40,4,600]{2,1,0:T(4,128)(2,1)S(1)} %pad_maximum_fusion), channel_id=1, source_target_pairs={{0,16},{8,24},{16,0},{24,8},{1,17},{9,25},{17,1},{25,9},{2,18},{10... | collective-permute-start | bytes 576008 | tf_op jit(solution)/shard_map/ppermute | solution.py:174
  12.9 13.7 %collective-permute-start.2 = (bf16[40,4,600]{2,1,0:T(4,128)(2,1)S(1)}, bf16[40,4,600]{2,1,0:T(4,128)(2,1)S(1)}, u32[]{:S(2)}, u32[]{:S(2)}) collective-permute-start(bf16[40,4,600]{2,1,0:T(4,128)(2,1)S(1)} %pad_maximum_fusion), channel_id=1, source_target_pairs={{0,8},{8,0},{16,24},{24,16},{1,9},{9,1},{17,25},{25,17},{2,10},{10... | collective-permute-start | bytes 576008 | tf_op jit(solution)/shard_map/ppermute | solution.py:174
  18.7 11.5 %collective-permute-start.9 = (bf16[40,4,600]{2,1,0:T(4,128)(2,1)S(1)}, bf16[40,4,600]{2,1,0:T(4,128)(2,1)S(1)}, u32[]{:S(2)}, u32[]{:S(2)}) collective-permute-start(bf16[40,4,600]{2,1,0:T(4,128)(2,1)S(1)} %pad_maximum_fusion.1), channel_id=1, source_target_pairs={{0,24},{8,16},{16,8},{24,0},{1,25},{9,17},{17,9},{25,1},{2,26},{10... | collective-permute-start | bytes 576008 | tf_op jit(solution)/shard_map/ppermute | solution.py:174
  21.3 9.3 %collective-permute-start.8 = (bf16[40,4,600]{2,1,0:T(4,128)(2,1)S(1)}, bf16[40,4,600]{2,1,0:T(4,128)(2,1)S(1)}, u32[]{:S(2)}, u32[]{:S(2)}) collective-permute-start(bf16[40,4,600]{2,1,0:T(4,128)(2,1)S(1)} %pad_maximum_fusion.1), channel_id=1, source_target_pairs={{0,16},{8,24},{16,0},{24,8},{1,17},{9,25},{17,1},{25,9},{2,18},{10... | collective-permute-start | bytes 576008 | tf_op jit(solution)/shard_map/ppermute | solution.py:174
  21.9 8.8 %collective-permute-start.7 = (bf16[40,4,600]{2,1,0:T(4,128)(2,1)S(1)}, bf16[40,4,600]{2,1,0:T(4,128)(2,1)S(1)}, u32[]{:S(2)}, u32[]{:S(2)}) collective-permute-start(bf16[40,4,600]{2,1,0:T(4,128)(2,1)S(1)} %pad_maximum_fusion.1), channel_id=1, source_target_pairs={{0,8},{8,0},{16,24},{24,16},{1,9},{9,1},{17,25},{25,17},{2,10},{10... | collective-permute-start | bytes 576008 | tf_op jit(solution)/shard_map/ppermute | solution.py:174
  22.4 0.7 %copy-start = (s32[600]{0:T(1024)S(1)}, s32[600]{0:T(1024)}, u32[]{:S(2)}) copy-start(s32[600]{0:T(1024)} %refs_1_.3) | copy-start | bytes 7204
  23.1 3.6 %copy-start.1 = (s32[600]{0:T(1024)S(1)}, s32[600]{0:T(1024)}, u32[]{:S(2)}) copy-start(s32[600]{0:T(1024)} %refs_1_.3) | copy-start | bytes 7204
  34.2 3.5 %collective-permute-start.10 = (f32[160,2432]{1,0:T(8,128)S(1)}, f32[160,2432]{1,0:T(8,128)S(1)}, u32[]{:S(2)}, u32[]{:S(2)}) collective-permute-start(f32[160,2432]{1,0:T(8,128)S(1)} %shard_map.40), channel_id=1, source_target_pairs={{0,1},{1,0},{2,3},{3,2},{4,5},{5,4},{6,7},{7,6},{8,9},{9,8},{10,11... | collective-permute-start | bytes 4669448 | tf_op jit(solution)/shard_map/ppermute | solution.py:174
  38.4 5.8 %collective-permute-start.14 = (s16[40,1280]{1,0:T(8,128)(2,1)S(1)}, s16[40,1280]{1,0:T(8,128)(2,1)S(1)}, u32[]{:S(2)}, u32[]{:S(2)}) collective-permute-start(s16[40,1280]{1,0:T(8,128)(2,1)S(1)} %get-tuple-element.44), channel_id=1, source_target_pairs={{0,2},{1,3},{2,0},{3,1},{4,6},{5,7},{6,4},{7,5},{8,10},{9,11},{10,... | collective-permute-start | bytes 307208 | tf_op jit(solution)/shard_map/ppermute | solution.py:174
  39.8 15.5 %collective-permute-start.11 = (s16[40,2432]{1,0:T(8,128)(2,1)S(1)}, s16[40,2432]{1,0:T(8,128)(2,1)S(1)}, u32[]{:S(2)}, u32[]{:S(2)}) collective-permute-start(s16[40,2432]{1,0:T(8,128)(2,1)S(1)} %get-tuple-element.40), channel_id=1, source_target_pairs={{0,2},{1,3},{2,0},{3,1},{4,6},{5,7},{6,4},{7,5},{8,10},{9,11},{10,... | collective-permute-start | bytes 583688 | tf_op jit(solution)/shard_map/ppermute | solution.py:174
  40.5 8.9 %collective-permute-start.12 = (s16[40,1280]{1,0:T(8,128)(2,1)S(1)}, s16[40,1280]{1,0:T(8,128)(2,1)S(1)}, u32[]{:S(2)}, u32[]{:S(2)}) collective-permute-start(s16[40,1280]{1,0:T(8,128)(2,1)S(1)} %get-tuple-element.41), channel_id=1, source_target_pairs={{0,4},{1,5},{2,6},{3,7},{4,0},{5,1},{6,2},{7,3},{8,12},{9,13},{10,... | collective-permute-start | bytes 307208 | tf_op jit(solution)/shard_map/ppermute | solution.py:174
  43.6 11.7 %collective-permute-start.13 = (s16[40,1280]{1,0:T(8,128)(2,1)S(1)}, s16[40,1280]{1,0:T(8,128)(2,1)S(1)}, u32[]{:S(2)}, u32[]{:S(2)}) collective-permute-start(s16[40,1280]{1,0:T(8,128)(2,1)S(1)} %get-tuple-element.42), channel_id=1, source_target_pairs={{0,6},{1,7},{2,4},{3,5},{4,2},{5,3},{6,0},{7,1},{8,14},{9,15},{10,... | collective-permute-start | bytes 307208 | tf_op jit(solution)/shard_map/ppermute | solution.py:174
  44.9 12.7 %collective-permute-start.15 = (s16[40,1280]{1,0:T(8,128)(2,1)S(1)}, s16[40,1280]{1,0:T(8,128)(2,1)S(1)}, u32[]{:S(2)}, u32[]{:S(2)}) collective-permute-start(s16[40,1280]{1,0:T(8,128)(2,1)S(1)} %shard_map.42), channel_id=1, source_target_pairs={{0,4},{1,5},{2,6},{3,7},{4,0},{5,1},{6,2},{7,3},{8,12},{9,13},{10,... | collective-permute-start | bytes 307208 | tf_op jit(solution)/shard_map/ppermute | solution.py:174

commit v5 on v4

--- a/solution.py
+++ b/solution.py
@@ -224,10 +224,9 @@
     y = in_order(got[chips // 2:])
     x_all = around(x)
     y, late, x_all[3] = lax.optimization_barrier((y, vvvv, x_all[3]))
-    parts = [mask(late, mem, 0, half // 2)]
-    x_all, parts, late = lax.optimization_barrier((x_all, parts, late))
-    y_all, part = lax.optimization_barrier((around(y), mask(late, mem, half // 2, half // 2)))
-    parts.append(part)
+    parts = [mask(late, mem, 0, half)]
+    x_all, parts = lax.optimization_barrier((x_all, parts))
+    y_all, parts = lax.optimization_barrier((around(y), parts))
     halves = [x_all, y_all]
 
     pair_rows = 2 * per_device

time: 58.9 us -> 58.6 us (level)
  waiting for transfers between devices: 16.1 us -> 22.1 us
  starting transfers between devices: 22.2 us -> 19.3 us
  Pallas kernels: 15.3 us -> 13.5 us
  local copies, waits for them, and re-layouts: 3.49 us -> 2.13 us
    ppermute x16, waiting for transfers between devices: 16.1 us -> 22.1 us  [swap(): return lax.ppermute(x, axis, [(i, i ^ k) for i in range(count)])]
    ppermute x16, starting transfers between devices: 22.2 us -> 19.3 us  [swap(): return lax.ppermute(x, axis, [(i, i ^ k) for i in range(count)])]
    pallas_call x2 -> x1, Pallas kernels: 7.13 us -> 5.28 us  [mask(): pl.pallas_call(lambda *refs: mask_kernel(base, *refs), in_specs=[SMEM, SM...]
    unnamed x12 -> x10, local copies, waits for them, and re-layouts: 0.89 us -> 0.21 us
    reshape x1, local copies, waits for them, and re-layouts: 0.69 us -> 0.01 us  [mask(): irreps.reshape(1, nv)]
  transfers between devices with their start and end apart: 16 -> 16, of which waited for: 10 -> 11; matrix products, arithmetic and copies ran while one was open for 3% -> 2% of each run, Pallas kernels for 18% -> 15%
where the time goes in v5:
time: 58.6 us; the launch traced here: 58.5 us
  waiting for transfers between devices  22.1 us (38%)
  starting transfers between devices  19.3 us (33%)
  Pallas kernels  13.5 us (23%)
  local copies, waits for them, and re-layouts  2.13 us (4%)
  other arithmetic  1.22 us (2%)
    ppermute x16, waiting for transfers between devices, swap(): return lax.ppermute(x, axis, [(i, i ^ k) for i in range(count)])  22.1 us
    ppermute x16, starting transfers between devices, swap(): return lax.ppermute(x, axis, [(i, i ^ k) for i in range(count)])  19.3 us
    pallas_call x2, Pallas kernels, multiply(): pl.pallas_call(lambda *refs: dot_kernel(grp_count, *refs), in_specs=[SMEM...  5.66 us
    pallas_call x1, Pallas kernels, mask(): pl.pallas_call(lambda *refs: mask_kernel(base, *refs), in_specs=[SMEM, SM...  5.28 us
  transfers between devices with their start and end apart: 16, of which 11 were waited for; matrix products, arithmetic and copies ran while one was open for 2% of the time, Pallas kernels for 15%

profile of v5, /device:TPU:0, one launch (start us, length us, event | category | flops | bytes accessed | tf_op | source)
XLA Modules:
  0.0 58.5 jit_solution(14084505710766291098)
XLA Ops:
  0.0 1.1 %reshape.33 = bf16[10,4,2,4,600]{4,3,2,1,0:T(4,128)(2,1)S(1)} reshape(bf16[10,32,600]{2,1,0:T(8,128)(2,1)} %param.3) | data formatting | bytes 768000 | tf_op jit(solution)/shard_map/reshape | solution.py:197
  1.7 1.1 %collective-permute-done = bf16[10,4,4,600]{3,2,1,0:T(4,128)(2,1)S(1)} collective-permute-done((bf16[10,4,4,600]{3,2,1,0:T(4,128)(2,1)S(1)}, bf16[10,4,4,600]{3,2,1,0:T(4,128)(2,1)S(1)}, u32[]{:S(2)}, u32[]{:S(2)}) %collective-permute-start) | collective-permute-done | bytes 192032 | tf_op jit(solution)/shard_map/ppermute | solution.py:174
  3.2 3.0 %collective-permute-start.1 = (bf16[20,4,600]{2,1,0:T(4,128)(2,1)S(1)}, bf16[20,4,600]{2,1,0:T(4,128)(2,1)S(1)}, u32[]{:S(2)}, u32[]{:S(2)}) collective-permute-start(bf16[20,4,600]{2,1,0:T(4,128)(2,1)S(1)} %get-tuple-element.56), channel_id=1, source_target_pairs={{0,2},{1,3},{2,0},{3,1},{4,6},{5,7},{6,4},{7,5},{8,10},{9,11},{10,... | collective-permute-start | bytes 288008 | tf_op jit(solution)/shard_map/ppermute | solution.py:174
  6.2 2.5 %collective-permute-start.4 = (bf16[20,4,600]{2,1,0:T(4,128)(2,1)S(1)}, bf16[20,4,600]{2,1,0:T(4,128)(2,1)S(1)}, u32[]{:S(2)}, u32[]{:S(2)}) collective-permute-start(bf16[20,4,600]{2,1,0:T(4,128)(2,1)S(1)} %get-tuple-element.55), channel_id=1, source_target_pairs={{0,6},{1,7},{2,4},{3,5},{4,2},{5,3},{6,0},{7,1},{8,14},{9,15},{10,... | collective-permute-start | bytes 288008 | tf_op jit(solution)/shard_map/ppermute | solution.py:174
  9.8 2.7 %collective-permute-start.6 = (bf16[40,4,600]{2,1,0:T(4,128)(2,1)S(1)}, bf16[40,4,600]{2,1,0:T(4,128)(2,1)S(1)}, u32[]{:S(2)}, u32[]{:S(2)}) collective-permute-start(bf16[40,4,600]{2,1,0:T(4,128)(2,1)S(1)} %pad_maximum_fusion), channel_id=1, source_target_pairs={{0,24},{8,16},{16,8},{24,0},{1,25},{9,17},{17,9},{25,1},{2,26},{10... | collective-permute-start | bytes 576008 | tf_op jit(solution)/shard_map/ppermute | solution.py:174
  13.3 1.4 %collective-permute-done.4 = bf16[20,4,600]{2,1,0:T(4,128)(2,1)S(1)} collective-permute-done((bf16[20,4,600]{2,1,0:T(4,128)(2,1)S(1)}, bf16[20,4,600]{2,1,0:T(4,128)(2,1)S(1)}, u32[]{:S(2)}, u32[]{:S(2)}) %collective-permute-start.4) | collective-permute-done | bytes 96032 | tf_op jit(solution)/shard_map/ppermute | solution.py:174
  14.7 3.6 %collective-permute-done.5 = bf16[20,4,600]{2,1,0:T(4,128)(2,1)S(1)} collective-permute-done((bf16[20,4,600]{2,1,0:T(4,128)(2,1)S(1)}, bf16[20,4,600]{2,1,0:T(4,128)(2,1)S(1)}, u32[]{:S(2)}, u32[]{:S(2)}) %collective-permute-start.5) | collective-permute-done | bytes 96032 | tf_op jit(solution)/shard_map/ppermute | solution.py:174
  18.8 2.6 %collective-permute-start.9 = (bf16[40,4,600]{2,1,0:T(4,128)(2,1)S(1)}, bf16[40,4,600]{2,1,0:T(4,128)(2,1)S(1)}, u32[]{:S(2)}, u32[]{:S(2)}) collective-permute-start(bf16[40,4,600]{2,1,0:T(4,128)(2,1)S(1)} %pad_maximum_fusion.1), channel_id=1, source_target_pairs={{0,24},{8,16},{16,8},{24,0},{1,25},{9,17},{17,9},{25,1},{2,26},{10... | collective-permute-start | bytes 576008 | tf_op jit(solution)/shard_map/ppermute | solution.py:174
  21.4 0.5 collective-permute-start.8
  22.4 5.3 %shard_map.37.refs_5_ = bf16[4,640,2432]{2,1,0:T(8,128)(2,1)S(1)} custom-call(s32[2]{0:T(128)S(1)} %pad_add_fusion.1.refs_0_, s32[600]{0:T(1024)S(1)} %copy-done, s32[1,600]{1,0:T(1,128)S(1)} %reshape.34.refs_2_, bf16[4,600,2400]{2,1,0:T(8,128)(2,1)} %bitcast.67), custom_call_target="tpu_custom_call" | custom-call | bytes 23040000 | tf_op jit(solution)/shard_map/pallas_call | solution.py:181
  27.7 2.9 %collective-permute-done.8 = bf16[40,4,600]{2,1,0:T(4,128)(2,1)S(1)} collective-permute-done((bf16[40,4,600]{2,1,0:T(4,128)(2,1)S(1)}, bf16[40,4,600]{2,1,0:T(4,128)(2,1)S(1)}, u32[]{:S(2)}, u32[]{:S(2)}) %collective-permute-start.8) | collective-permute-done | bytes 192032 | tf_op jit(solution)/shard_map/ppermute | solution.py:174
  31.4 2.8 %shard_map.39 = f32[160,2432]{1,0:T(8,128)S(1)} custom-call(s32[3]{0:T(128)S(1)} %pad_add_fusion.refs_0_, bf16[40,2560]{1,0:T(8,128)(2,1)S(1)} %bitcast.63, bf16[40,2560]{1,0:T(8,128)(2,1)S(1)} %bitcast.64, bf16[40,2560]{1,0:T(8,128)(2,1)S(1)} %bitcast.59, bf16[40,2560]{1,0:T(8,128)(2,1)S(1)} %bitcast.66, bf16[4,640,2432]{2,1,0:T(8,128)(2,1)S(1)} %shard_map.37.refs_5_), custom_call_target="tpu_custom_call" | custom-call | flops 1843200000 | bytes 1536000 | tf_op jit(solution)/shard_map/pallas_call | solution.py:254
  34.8 2.8 %shard_map.38.refs_0_ = f32[160,2432]{1,0:T(8,128)S(1)} custom-call(s32[3]{0:T(128)S(1)} %pad_add_fusion.refs_0_, bf16[40,2560]{1,0:T(8,128)(2,1)S(1)} %bitcast.61, bf16[40,2560]{1,0:T(8,128)(2,1)S(1)} %bitcast.62, bf16[40,2560]{1,0:T(8,128)(2,1)S(1)} %bitcast.60, bf16[40,2560]{1,0:T(8,128)(2,1)S(1)} %bitcast.65, bf16[4,640,2432]{2,1,0:T(8,128)(2,1)S(1)} %shard_map.37.refs_5_), custom_call_target="tpu_custom_call" | custom-call | flops 1843200000 | bytes 1536000 | tf_op jit(solution)/shard_map/pallas_call | solution.py:254
  37.7 0.7 %shard_map.40 = (f32[40,2432]{1,0:T(8,128)S(1)}, s16[40,2432]{1,0:T(8,128)(2,1)S(1)}, s16[40,1280]{1,0:T(8,128)(2,1)S(1)}, s16[40,1280]{1,0:T(8,128)(2,1)S(1)}, ...) custom-call(f32[160,2432]{1,0:T(8,128)S(1)} %shard_map.38.refs_0_, f32[160,2432]{1,0:T(8,128)S(1)} %collective-permute-done.10.refs_1_), custom_call_target="tpu_custom_call" | custom-call | tf_op jit(solution)/shard_map/pallas_call | solution.py:267
  38.4 1.4 %collective-permute-start.14 = (s16[40,1280]{1,0:T(8,128)(2,1)S(1)}, s16[40,1280]{1,0:T(8,128)(2,1)S(1)}, u32[]{:S(2)}, u32[]{:S(2)}) collective-permute-start(s16[40,1280]{1,0:T(8,128)(2,1)S(1)} %get-tuple-element.42), channel_id=1, source_target_pairs={{0,2},{1,3},{2,0},{3,1},{4,6},{5,7},{6,4},{7,5},{8,10},{9,11},{10,... | collective-permute-start | bytes 307208 | tf_op jit(solution)/shard_map/ppermute | solution.py:174
  39.8 0.7 %collective-permute-start.11 = (s16[40,2432]{1,0:T(8,128)(2,1)S(1)}, s16[40,2432]{1,0:T(8,128)(2,1)S(1)}, u32[]{:S(2)}, u32[]{:S(2)}) collective-permute-start(s16[40,2432]{1,0:T(8,128)(2,1)S(1)} %get-tuple-element.38), channel_id=1, source_target_pairs={{0,2},{1,3},{2,0},{3,1},{4,6},{5,7},{6,4},{7,5},{8,10},{9,11},{10,... | collective-permute-start | bytes 583688 | tf_op jit(solution)/shard_map/ppermute | solution.py:174
  40.5 2.4 %collective-permute-start.12 = (s16[40,1280]{1,0:T(8,128)(2,1)S(1)}, s16[40,1280]{1,0:T(8,128)(2,1)S(1)}, u32[]{:S(2)}, u32[]{:S(2)}) collective-permute-start(s16[40,1280]{1,0:T(8,128)(2,1)S(1)} %get-tuple-element.39), channel_id=1, source_target_pairs={{0,4},{1,5},{2,6},{3,7},{4,0},{5,1},{6,2},{7,3},{8,12},{9,13},{10,... | collective-permute-start | bytes 307208 | tf_op jit(solution)/shard_map/ppermute | solution.py:174
  42.8 1.3 %collective-permute-start.13 = (s16[40,1280]{1,0:T(8,128)(2,1)S(1)}, s16[40,1280]{1,0:T(8,128)(2,1)S(1)}, u32[]{:S(2)}, u32[]{:S(2)}) collective-permute-start(s16[40,1280]{1,0:T(8,128)(2,1)S(1)} %get-tuple-element.40), channel_id=1, source_target_pairs={{0,6},{1,7},{2,4},{3,5},{4,2},{5,3},{6,0},{7,1},{8,14},{9,15},{10,... | collective-permute-start | bytes 307208 | tf_op jit(solution)/shard_map/ppermute | solution.py:174
  44.2 2.1 %collective-permute-done.14.refs_1_ = s16[40,1280]{1,0:T(8,128)(2,1)S(1)} collective-permute-done((s16[40,1280]{1,0:T(8,128)(2,1)S(1)}, s16[40,1280]{1,0:T(8,128)(2,1)S(1)}, u32[]{:S(2)}, u32[]{:S(2)}) %collective-permute-start.14) | collective-permute-done | bytes 102432 | tf_op jit(solution)/shard_map/ppermute | solution.py:174
  46.3 0.7 %shard_map.41 = s16[40,1280]{1,0:T(8,128)(2,1)S(1)} custom-call(f32[40,1280]{1,0:T(8,128)S(1)} %get-tuple-element.41.refs_0_, s16[40,1280]{1,0:T(8,128)(2,1)S(1)} %collective-permute-done.14.refs_1_), custom_call_target="tpu_custom_call" | custom-call | tf_op jit(solution)/shard_map/pallas_call | solution.py:287
  47.3 2.1 %collective-permute-done.12.refs_2_ = s16[40,1280]{1,0:T(8,128)(2,1)S(1)} collective-permute-done((s16[40,1280]{1,0:T(8,128)(2,1)S(1)}, s16[40,1280]{1,0:T(8,128)(2,1)S(1)}, u32[]{:S(2)}, u32[]{:S(2)}) %collective-permute-start.12) | collective-permute-done | bytes 102432 | tf_op jit(solution)/shard_map/ppermute | solution.py:174
  49.4 5.2 %collective-permute-done.13.refs_3_ = s16[40,1280]{1,0:T(8,128)(2,1)S(1)} collective-permute-done((s16[40,1280]{1,0:T(8,128)(2,1)S(1)}, s16[40,1280]{1,0:T(8,128)(2,1)S(1)}, u32[]{:S(2)}, u32[]{:S(2)}) %collective-permute-start.13) | collective-permute-done | bytes 102432 | tf_op jit(solution)/shard_map/ppermute | solution.py:174
  54.6 2.8 %collective-permute-done.15.refs_4_ = s16[40,1280]{1,0:T(8,128)(2,1)S(1)} collective-permute-done((s16[40,1280]{1,0:T(8,128)(2,1)S(1)}, s16[40,1280]{1,0:T(8,128)(2,1)S(1)}, u32[]{:S(2)}, u32[]{:S(2)}) %collective-permute-start.15) | collective-permute-done | bytes 102432 | tf_op jit(solution)/shard_map/ppermute | solution.py:174
  57.4 1.1 %shard_map.42 = f32[40,2400]{1,0:T(8,128)} custom-call(f32[40,2432]{1,0:T(8,128)S(1)} %get-tuple-element.37.refs_0_, s16[40,2432]{1,0:T(8,128)(2,1)S(1)} %collective-permute-done.11.refs_1_, s16[40,1280]{1,0:T(8,128)(2,1)S(1)} %collective-permute-done.12.refs_2_, s16[40,1280]{1,0:T(8,128)(2,1)S(1)} %collective-permute-done.13.refs_3_, ...), custom_call_target="tpu_custom_call" | custom-call | tf_op jit(solution)/shard_map/pallas_call | solution.py:295
  (46 shorter events, 5.4 us)
Async XLA Ops:
  0.0 6.2 %copy-start = (s32[600]{0:T(1024)S(1)}, s32[600]{0:T(1024)}, u32[]{:S(2)}) copy-start(s32[600]{0:T(1024)} %refs_1_.1) | copy-start | bytes 7204
  1.2 1.6 %collective-permute-start = (bf16[10,4,4,600]{3,2,1,0:T(4,128)(2,1)S(1)}, bf16[10,4,4,600]{3,2,1,0:T(4,128)(2,1)S(1)}, u32[]{:S(2)}, u32[]{:S(2)}) collective-permute-start(bf16[10,4,4,600]{3,2,1,0:T(4,128)(2,1)S(1)} %dynamic-slice_bitcast_fusion), channel_id=1, source_target_pairs={{0,1},{1,0},{2,3},{3,2},{4,5},{5,4},{6,7},{7,6},{8,9},{9,8},{10,11... | collective-permute-start | bytes 576008 | tf_op jit(solution)/shard_map/ppermute | solution.py:174
  3.2 6.2 %collective-permute-start.1 = (bf16[20,4,600]{2,1,0:T(4,128)(2,1)S(1)}, bf16[20,4,600]{2,1,0:T(4,128)(2,1)S(1)}, u32[]{:S(2)}, u32[]{:S(2)}) collective-permute-start(bf16[20,4,600]{2,1,0:T(4,128)(2,1)S(1)} %get-tuple-element.56), channel_id=1, source_target_pairs={{0,2},{1,3},{2,0},{3,1},{4,6},{5,7},{6,4},{7,5},{8,10},{9,11},{10,... | collective-permute-start | bytes 288008 | tf_op jit(solution)/shard_map/ppermute | solution.py:174
  6.2 8.5 %collective-permute-start.4 = (bf16[20,4,600]{2,1,0:T(4,128)(2,1)S(1)}, bf16[20,4,600]{2,1,0:T(4,128)(2,1)S(1)}, u32[]{:S(2)}, u32[]{:S(2)}) collective-permute-start(bf16[20,4,600]{2,1,0:T(4,128)(2,1)S(1)} %get-tuple-element.55), channel_id=1, source_target_pairs={{0,6},{1,7},{2,4},{3,5},{4,2},{5,3},{6,0},{7,1},{8,14},{9,15},{10,... | collective-permute-start | bytes 288008 | tf_op jit(solution)/shard_map/ppermute | solution.py:174
  8.7 9.6 %collective-permute-start.5 = (bf16[20,4,600]{2,1,0:T(4,128)(2,1)S(1)}, bf16[20,4,600]{2,1,0:T(4,128)(2,1)S(1)}, u32[]{:S(2)}, u32[]{:S(2)}) collective-permute-start(bf16[20,4,600]{2,1,0:T(4,128)(2,1)S(1)} %get-tuple-element.57), channel_id=1, source_target_pairs={{0,4},{1,5},{2,6},{3,7},{4,0},{5,1},{6,2},{7,3},{8,12},{9,13},{10,... | collective-permute-start | bytes 288008 | tf_op jit(solution)/shard_map/ppermute | solution.py:174
  9.8 9.0 %collective-permute-start.6 = (bf16[40,4,600]{2,1,0:T(4,128)(2,1)S(1)}, bf16[40,4,600]{2,1,0:T(4,128)(2,1)S(1)}, u32[]{:S(2)}, u32[]{:S(2)}) collective-permute-start(bf16[40,4,600]{2,1,0:T(4,128)(2,1)S(1)} %pad_maximum_fusion), channel_id=1, source_target_pairs={{0,24},{8,16},{16,8},{24,0},{1,25},{9,17},{17,9},{25,1},{2,26},{10... | collective-permute-start | bytes 576008 | tf_op jit(solution)/shard_map/ppermute | solution.py:174
  12.4 15.3 %collective-permute-start.3 = (bf16[40,4,600]{2,1,0:T(4,128)(2,1)S(1)}, bf16[40,4,600]{2,1,0:T(4,128)(2,1)S(1)}, u32[]{:S(2)}, u32[]{:S(2)}) collective-permute-start(bf16[40,4,600]{2,1,0:T(4,128)(2,1)S(1)} %pad_maximum_fusion), channel_id=1, source_target_pairs={{0,16},{8,24},{16,0},{24,8},{1,17},{9,25},{17,1},{25,9},{2,18},{10... | collective-permute-start | bytes 576008 | tf_op jit(solution)/shard_map/ppermute | solution.py:174
  12.9 14.8 %collective-permute-start.2 = (bf16[40,4,600]{2,1,0:T(4,128)(2,1)S(1)}, bf16[40,4,600]{2,1,0:T(4,128)(2,1)S(1)}, u32[]{:S(2)}, u32[]{:S(2)}) collective-permute-start(bf16[40,4,600]{2,1,0:T(4,128)(2,1)S(1)} %pad_maximum_fusion), channel_id=1, source_target_pairs={{0,8},{8,0},{16,24},{24,16},{1,9},{9,1},{17,25},{25,17},{2,10},{10... | collective-permute-start | bytes 576008 | tf_op jit(solution)/shard_map/ppermute | solution.py:174
  18.8 8.9 %collective-permute-start.9 = (bf16[40,4,600]{2,1,0:T(4,128)(2,1)S(1)}, bf16[40,4,600]{2,1,0:T(4,128)(2,1)S(1)}, u32[]{:S(2)}, u32[]{:S(2)}) collective-permute-start(bf16[40,4,600]{2,1,0:T(4,128)(2,1)S(1)} %pad_maximum_fusion.1), channel_id=1, source_target_pairs={{0,24},{8,16},{16,8},{24,0},{1,25},{9,17},{17,9},{25,1},{2,26},{10... | collective-permute-start | bytes 576008 | tf_op jit(solution)/shard_map/ppermute | solution.py:174
  21.4 9.2 %collective-permute-start.8 = (bf16[40,4,600]{2,1,0:T(4,128)(2,1)S(1)}, bf16[40,4,600]{2,1,0:T(4,128)(2,1)S(1)}, u32[]{:S(2)}, u32[]{:S(2)}) collective-permute-start(bf16[40,4,600]{2,1,0:T(4,128)(2,1)S(1)} %pad_maximum_fusion.1), channel_id=1, source_target_pairs={{0,16},{8,24},{16,0},{24,8},{1,17},{9,25},{17,1},{25,9},{2,18},{10... | collective-permute-start | bytes 576008 | tf_op jit(solution)/shard_map/ppermute | solution.py:174
  21.9 8.8 %collective-permute-start.7 = (bf16[40,4,600]{2,1,0:T(4,128)(2,1)S(1)}, bf16[40,4,600]{2,1,0:T(4,128)(2,1)S(1)}, u32[]{:S(2)}, u32[]{:S(2)}) collective-permute-start(bf16[40,4,600]{2,1,0:T(4,128)(2,1)S(1)} %pad_maximum_fusion.1), channel_id=1, source_target_pairs={{0,8},{8,0},{16,24},{24,16},{1,9},{9,1},{17,25},{25,17},{2,10},{10... | collective-permute-start | bytes 576008 | tf_op jit(solution)/shard_map/ppermute | solution.py:174
  34.2 3.5 %collective-permute-start.10 = (f32[160,2432]{1,0:T(8,128)S(1)}, f32[160,2432]{1,0:T(8,128)S(1)}, u32[]{:S(2)}, u32[]{:S(2)}) collective-permute-start(f32[160,2432]{1,0:T(8,128)S(1)} %shard_map.39), channel_id=1, source_target_pairs={{0,1},{1,0},{2,3},{3,2},{4,5},{5,4},{6,7},{7,6},{8,9},{9,8},{10,11... | collective-permute-start | bytes 4669448 | tf_op jit(solution)/shard_map/ppermute | solution.py:174
  38.4 7.9 %collective-permute-start.14 = (s16[40,1280]{1,0:T(8,128)(2,1)S(1)}, s16[40,1280]{1,0:T(8,128)(2,1)S(1)}, u32[]{:S(2)}, u32[]{:S(2)}) collective-permute-start(s16[40,1280]{1,0:T(8,128)(2,1)S(1)} %get-tuple-element.42), channel_id=1, source_target_pairs={{0,2},{1,3},{2,0},{3,1},{4,6},{5,7},{6,4},{7,5},{8,10},{9,11},{10,... | collective-permute-start | bytes 307208 | tf_op jit(solution)/shard_map/ppermute | solution.py:174
  39.8 14.8 %collective-permute-start.11 = (s16[40,2432]{1,0:T(8,128)(2,1)S(1)}, s16[40,2432]{1,0:T(8,128)(2,1)S(1)}, u32[]{:S(2)}, u32[]{:S(2)}) collective-permute-start(s16[40,2432]{1,0:T(8,128)(2,1)S(1)} %get-tuple-element.38), channel_id=1, source_target_pairs={{0,2},{1,3},{2,0},{3,1},{4,6},{5,7},{6,4},{7,5},{8,10},{9,11},{10,... | collective-permute-start | bytes 583688 | tf_op jit(solution)/shard_map/ppermute | solution.py:174
  40.5 8.9 %collective-permute-start.12 = (s16[40,1280]{1,0:T(8,128)(2,1)S(1)}, s16[40,1280]{1,0:T(8,128)(2,1)S(1)}, u32[]{:S(2)}, u32[]{:S(2)}) collective-permute-start(s16[40,1280]{1,0:T(8,128)(2,1)S(1)} %get-tuple-element.39), channel_id=1, source_target_pairs={{0,4},{1,5},{2,6},{3,7},{4,0},{5,1},{6,2},{7,3},{8,12},{9,13},{10,... | collective-permute-start | bytes 307208 | tf_op jit(solution)/shard_map/ppermute | solution.py:174
  42.8 11.7 %collective-permute-start.13 = (s16[40,1280]{1,0:T(8,128)(2,1)S(1)}, s16[40,1280]{1,0:T(8,128)(2,1)S(1)}, u32[]{:S(2)}, u32[]{:S(2)}) collective-permute-start(s16[40,1280]{1,0:T(8,128)(2,1)S(1)} %get-tuple-element.40), channel_id=1, source_target_pairs={{0,6},{1,7},{2,4},{3,5},{4,2},{5,3},{6,0},{7,1},{8,14},{9,15},{10,... | collective-permute-start | bytes 307208 | tf_op jit(solution)/shard_map/ppermute | solution.py:174
  47.0 10.3 %collective-permute-start.15 = (s16[40,1280]{1,0:T(8,128)(2,1)S(1)}, s16[40,1280]{1,0:T(8,128)(2,1)S(1)}, u32[]{:S(2)}, u32[]{:S(2)}) collective-permute-start(s16[40,1280]{1,0:T(8,128)(2,1)S(1)} %shard_map.41), channel_id=1, source_target_pairs={{0,4},{1,5},{2,6},{3,7},{4,0},{5,1},{6,2},{7,3},{8,12},{9,13},{10,... | collective-permute-start | bytes 307208 | tf_op jit(solution)/shard_map/ppermute | solution.py:174
